TPU v7x, 512 devices: a whole 4x8x8 slice. The times are simulated.
512 devices in a mesh: dom: 16 (over x, y_lo, core), orb: 32 (over z, y_hi).
Axes of the slice: x: 4, y: 8 (y_hi: 4, y_lo: 2; y = y_hi * 2 + y_lo), z: 8, core: 2. Of those that a mesh axis runs over, the one named last changes fastest.
Arguments:
- orbitals: float32 [16, 64, 48, 2304], P('dom', 'orb'), may hold values from -6 to 6
- occupations: float32 [16, 64], P('dom', 'orb'), may hold values from 0.25 to 2
- occupied_count: int32 [16], P('dom'), may hold values from 16 to 64
- weights: float32 [16, 48], P('dom'), may hold values from 0 to 1, as said below
- external_potential: float32 [16, 48, 2304], P('dom'), may hold values from -2 to 0.5
- core_density: float32 [16, 48, 2304], P('dom'), may hold values from 0.08 to 2.88, as said below
- hartree_guess: float32 [512, 2304], P(('dom', 'orb')), may hold values from -6 to 6
Outputs:
- potential: float32 [512, 2304], P(('dom', 'orb'))
Inputs may be any that keep to these rules, and one draw needn't show every extreme that they name: orbitals 0 to occupied_count - 1 of a domain are occupied. `weights`: positive; on every global plane the weights of the boxes that cover it sum to one. `core_density`: positive.
All inputs are finite; a program needn't handle non-finite values.
Results may differ from a plain program's by a relative error of at most 0.00017.
Values sent between devices are 32-bit elements; how exact they have to be, the bound alone decides.
No kernel may reach another device: no remote copies, remote signals or barrier semaphores. Data moves between devices by JAX's collectives and lax.ppermute only.
A program may use at most 64 MiB of HBM per device.

v0:
```python
import functools

import jax
import jax.numpy as jnp
from jax import lax
from jax.experimental import pallas as pl
from jax.experimental.pallas import tpu as pltpu
from jax.sharding import PartitionSpec as P

SIDE = 48
CORE = 32
BUF = 8
DEGREE = 8
SWEEPS = 4
BOX = 48
CELLS = SIDE * SIDE
LANES = 128
COLS = CELLS // LANES
PAD = 8
EXT = 64

EXCHANGE_FACTOR = (3.0 / 3.141592653589793) ** (1.0 / 3.0)
FOUR_PI = 4.0 * 3.141592653589793
RELAXATION = 0.8
CUTOFF = 1.5
KEEP = 1.0 - RELAXATION
SPREAD = RELAXATION / 6.0
SOURCE = SPREAD * FOUR_PI


def masks():
    lane = lax.broadcasted_iota(jnp.int32, (8, LANES), 1)
    row = lax.broadcasted_iota(jnp.int32, (8, LANES), 0)
    first = [(lane + LANES * i) % SIDE == 0 for i in range(3)]
    last = [(lane + LANES * i) % SIDE == SIDE - 1 for i in range(3)]
    return dict(lane=lane, row=row, first=first, last=last)


def shifted(pieces, shift, m):
    whole, part = divmod(shift, LANES)
    turned = [pltpu.roll(p, part, 1) for p in pieces]
    keep = m["lane"] >= part
    n = len(pieces)
    return [jnp.where(keep, turned[(i - whole) % n], turned[(i - whole - 1) % n]) for i in range(n)]


def neighbour_sum(above, here, below, m):
    left = shifted(here, 1, m)
    right = shifted(here, -1, m)
    left_wrap = [jnp.where(m["first"][i % 3], left[i], 0.0) for i in range(COLS)]
    left_rest = [jnp.where(m["first"][i % 3], 0.0, left[i]) for i in range(COLS)]
    right_wrap = [jnp.where(m["last"][i % 3], right[i], 0.0) for i in range(COLS)]
    right_rest = [jnp.where(m["last"][i % 3], 0.0, right[i]) for i in range(COLS)]
    down = shifted([here[i] + left_wrap[i] for i in range(COLS)], -SIDE, m)
    up = shifted([here[i] + right_wrap[i] for i in range(COLS)], SIDE, m)
    out = []
    for i in range(COLS):
        before = pltpu.roll(jnp.where(m["row"] == 7, above[i], here[i]), 1, 0)
        after = pltpu.roll(jnp.where(m["row"] == 0, below[i], here[i]), 7, 0)
        out.append(((left_rest[i] + right_rest[i]) + (down[i] + up[i])) + (before + after))
    return out


def pieces_of(ref, lead, start):
    rows = pl.ds(start if isinstance(start, int) else pl.multiple_of(start, 8), 8)
    return [ref[(*lead, rows, pl.ds(LANES * i, LANES))] for i in range(COLS)]


def put_pieces(ref, lead, start, pieces):
    rows = pl.ds(start if isinstance(start, int) else pl.multiple_of(start, 8), 8)
    for i in range(COLS):
        ref[(*lead, rows, pl.ds(LANES * i, LANES))] = pieces[i]


def sum_at(ref, lead, start, m):
    above, here, below = (pieces_of(ref, lead, start + k) for k in (-8, 0, 8))
    return here, neighbour_sum(above, here, below, m)


def run_filter(psi_ref, a_ref, b_ref, w_ref, v_tile, m):
    orbs = psi_ref.shape[0]
    low = high = None
    for t in range(BOX // 8):
        for v in v_tile(8 * t):
            low = v if low is None else jnp.minimum(low, v)
            high = v if high is None else jnp.maximum(high, v)
    low = jnp.min(low, keepdims=True) + CUTOFF
    high = jnp.max(high, keepdims=True) + 6.0
    center = 0.5 * (high + low)
    inverse = 1.0 / (0.5 * (high - low))
    offset = (3.0 - center) * (2.0 * inverse)
    double = jnp.broadcast_to(2.0 * inverse, (8, LANES))
    single = jnp.broadcast_to(inverse, (8, LANES))
    offset = jnp.broadcast_to(offset, (8, LANES))
    for t in range(BOX // 8):
        put_pieces(w_ref, (), 8 * t, [double * v + offset for v in v_tile(8 * t)])
    zero = jnp.zeros((PAD, CELLS), jnp.float32)
    for q in range(orbs):
        for ref in (a_ref, b_ref):
            ref[q, 0:PAD, :] = zero
            ref[q, PAD + BOX : PAD + BOX + PAD, :] = zero
        a_ref[q, PAD : PAD + BOX, :] = psi_ref[q]

    def step(source, target, first):
        def tile(t, carry):
            w = pieces_of(w_ref, (), 8 * t)
            for q in range(orbs):
                here, around = sum_at(source, (q,), PAD + 8 * t, m)
                new = [w[i] * here[i] - single * around[i] for i in range(COLS)]
                if first:
                    new = [0.5 * n for n in new]
                else:
                    old = pieces_of(target, (q,), PAD + 8 * t)
                    new = [new[i] - old[i] for i in range(COLS)]
                put_pieces(target, (q,), PAD + 8 * t, new)
            return carry

        lax.fori_loop(0, BOX // 8, tile, 0)

    step(a_ref, b_ref, True)

    def pair(k, carry):
        step(b_ref, a_ref, False)
        step(a_ref, b_ref, False)
        return carry

    lax.fori_loop(0, (DEGREE - 2) // 2, pair, 0)
    step(b_ref, a_ref, False)


def norms(a_ref, orbs):
    out = []
    for q in range(orbs):
        total = [jnp.zeros((8, LANES), jnp.float32) for _ in range(3)]
        for t in range(BOX // 8):
            for i, y in enumerate(pieces_of(a_ref, (q,), PAD + 8 * t)):
                total[i % 3] = total[i % 3] + y * y
        mean = jnp.sum(total[0] + total[1] + total[2], keepdims=True) * (1.0 / (BOX * CELLS))
        out.append(jnp.broadcast_to(lax.rsqrt(mean + 1e-06), (8, LANES)))
    return out


def density_tile(a_ref, scale, factor_ref, core_ref, weight_ref, t, share, psi_out):
    weight = jnp.broadcast_to(weight_ref[8 * t : 8 * t + 8, :], (8, LANES))
    total = [share * c for c in pieces_of(core_ref, (0,), 8 * t)]
    for q in range(len(scale)):
        y = [p * scale[q] for p in pieces_of(a_ref, (q,), PAD + 8 * t)]
        if psi_out is not None:
            put_pieces(psi_out, (q,), 8 * t, y)
        total = [total[i] + factor_ref[q] * (y[i] * y[i]) for i in range(COLS)]
    return [weight * d for d in total]


def first_kernel(share, factor_ref, psi_ref, ext_ref, core_ref, weight_ref, psi_out, own_out, up_out, a_ref, b_ref, w_ref):
    m = masks()
    run_filter(psi_ref.at[0], a_ref, b_ref, w_ref, lambda r: pieces_of(ext_ref, (0,), r), m)
    scale = norms(a_ref, psi_ref.shape[1])
    for t in range(BOX // 8):
        tile = density_tile(a_ref, scale, factor_ref, core_ref, weight_ref, t, share, psi_out)
        if t < 3:
            put_pieces(own_out, (), 8 * t, tile)
        else:
            put_pieces(up_out, (), 8 * (t - 3), tile)


def sweep(source, target, density, m):
    def tile(t, carry):
        here, around = sum_at(source, (), PAD + 8 * t, m)
        new = [KEEP * here[i] + SPREAD * around[i] for i in range(COLS)]
        if density is not None:
            push = pieces_of(density, (), 8 * t)
            new = [new[i] + SOURCE * push[i] for i in range(COLS)]
        put_pieces(target, (), PAD + 8 * t, new)
        return carry

    lax.fori_loop(0, EXT // 8, tile, 0)


def second_kernel(
    share, factor_ref, psi_ref, ext_ref, core_ref, weight_ref, before_ref, guess_ref, after_ref, low_ref, high_ref,
    hartree_out, core_out, smooth_out, up_out, down_out, charge_out,
    a_ref, b_ref, w_ref, g_ref, h_ref, d_ref,
):
    m = masks()
    orbs = psi_ref.shape[0]
    zero = jnp.zeros((PAD, CELLS), jnp.float32)
    for ref in (g_ref, h_ref):
        ref[0:PAD, :] = zero
        ref[PAD + EXT : PAD + EXT + PAD, :] = zero
    g_ref[PAD : PAD + 16, :] = before_ref[...]
    g_ref[PAD + 16 : PAD + 48, :] = guess_ref[...]
    g_ref[PAD + 48 : PAD + 64, :] = after_ref[...]
    d_ref[0:32, :] = low_ref[...]
    d_ref[32:64, :] = high_ref[...]
    for _ in range(SWEEPS // 2):
        sweep(g_ref, h_ref, d_ref, m)
        sweep(h_ref, g_ref, d_ref, m)
    hartree_out[...] = g_ref[PAD : PAD + EXT, :]
    charge = [jnp.zeros((8, LANES), jnp.float32) for _ in range(3)]
    for t in range(4):
        for i, d in enumerate(pieces_of(d_ref, (), 8 * t)):
            charge[i % 3] = charge[i % 3] + d
    frame_charge = (charge[0] + charge[1] + charge[2]) * share
    for t in range(BOX // 8):
        density = pieces_of(d_ref, (), 8 + 8 * t)
        hartree = pieces_of(g_ref, (), PAD + 8 + 8 * t)
        ionic = pieces_of(ext_ref, (0,), 8 * t)
        new = [
            ionic[i] + (hartree[i] - EXCHANGE_FACTOR * jnp.exp(jnp.log(density[i]) * (1.0 / 3.0)))
            for i in range(COLS)
        ]
        put_pieces(h_ref, (), PAD + 8 * t, new)
    run_filter(psi_ref, a_ref, b_ref, w_ref, lambda r: pieces_of(h_ref, (), PAD + r), m)
    scale = norms(a_ref, orbs)
    for ref in (g_ref, h_ref):
        ref[PAD : PAD + 8, :] = zero
        ref[PAD + 56 : PAD + 64, :] = zero
    d_ref[0:8, :] = zero
    d_ref[56:64, :] = zero
    charge = [frame_charge] + [jnp.zeros((8, LANES), jnp.float32) for _ in range(2)]
    for t in range(BOX // 8):
        tile = density_tile(a_ref, scale, factor_ref, core_ref, weight_ref, t, share, None)
        put_pieces(d_ref, (), 8 + 8 * t, tile)
        put_pieces(g_ref, (), PAD + 8 + 8 * t, [SOURCE * d for d in tile])
        if t == 0:
            put_pieces(down_out, (), 0, tile)
        elif t == 5:
            put_pieces(up_out, (), 0, tile)
        else:
            put_pieces(core_out, (), 8 * (t - 1), tile)
        for i, d in enumerate(tile):
            charge[i % 3] = charge[i % 3] + d
    charge_out[...] = jnp.broadcast_to(jnp.sum(charge[0] + charge[1] + charge[2], keepdims=True), charge_out.shape)
    sweep(g_ref, h_ref, d_ref, m)
    sweep(h_ref, g_ref, d_ref, m)
    sweep(g_ref, h_ref, d_ref, m)
    down_out[8:24, :] = h_ref[PAD : PAD + 16, :]
    smooth_out[...] = h_ref[PAD + 16 : PAD + 48, :]
    up_out[8:24, :] = h_ref[PAD + 48 : PAD + 64, :]


def decay_kernel(hartree_ref, out_ref, g_ref, h_ref):
    m = masks()
    zero = jnp.zeros((PAD, CELLS), jnp.float32)
    for ref in (g_ref, h_ref):
        ref[0:PAD, :] = zero
        ref[PAD + EXT : PAD + EXT + PAD, :] = zero
    g_ref[PAD : PAD + EXT, :] = hartree_ref[...]
    for _ in range(SWEEPS // 2):
        sweep(g_ref, h_ref, None, m)
        sweep(h_ref, g_ref, None, m)
    out_ref[...] = g_ref[PAD + 16 : PAD + 48, :]


VMEM = pl.BlockSpec(memory_space=pltpu.VMEM)
SMEM = pl.BlockSpec(memory_space=pltpu.SMEM)
LIMIT = pltpu.CompilerParams(vmem_limit_bytes=40 * 2**20)


def f32(*shape):
    return jax.ShapeDtypeStruct(shape, jnp.float32)


def body(orbitals, occupations, occupied_count, weights, external_potential, core_density, hartree_guess):
    orb_count = lax.axis_size("orb")
    dom_count = lax.axis_size("dom")
    orb_rank = lax.axis_index("orb")
    per_device = orbitals.shape[1]
    rank = orb_rank * per_device + jnp.arange(per_device, dtype=jnp.int32)
    factors = jnp.where(rank < occupied_count[0], occupations[0], jnp.float32(0.0)) / (per_device * orb_count)
    weight = weights.reshape(BOX, 1)
    share = 1.0 / orb_count
    up = [(i, (i + 1) % dom_count) for i in range(dom_count)]
    down = [(j, i) for i, j in up]
    filter_scratch = [
        pltpu.VMEM((per_device, BOX + 2 * PAD, CELLS), jnp.float32),
        pltpu.VMEM((per_device, BOX + 2 * PAD, CELLS), jnp.float32),
        pltpu.VMEM((BOX, CELLS), jnp.float32),
    ]
    field = pltpu.VMEM((EXT + 2 * PAD, CELLS), jnp.float32)

    psi, own, upper = pl.pallas_call(
        functools.partial(first_kernel, share),
        in_specs=[SMEM] + [VMEM] * 4,
        out_specs=[VMEM] * 3,
        out_shape=[f32(per_device, BOX, CELLS), f32(24, CELLS), f32(24, CELLS)],
        scratch_shapes=filter_scratch,
        compiler_params=LIMIT,
        name="first",
    )(factors, orbitals, external_potential, core_density, weight)

    behind = lax.ppermute(upper, "dom", up)
    frame = jnp.concatenate([behind[:8], own[:16] + behind[8:], own[16:]], axis=0)
    sent = jnp.concatenate(
        [frame[:, None], jnp.broadcast_to(hartree_guess[None], (orb_count, 1, CELLS))], axis=2
    )
    arrived = lax.all_to_all(sent, "orb", 0, 0, tiled=True)
    plane = arrived[:, :, :CELLS].sum(axis=0)
    guess = arrived[:, 0, CELLS:]
    guess_before = lax.ppermute(guess[16:], "dom", up)
    guess_after = lax.ppermute(guess[:16], "dom", down)
    low = lax.all_to_all(jnp.broadcast_to(plane[None], (orb_count, 1, CELLS)), "orb", 0, 0, tiled=True)
    low = low.reshape(CORE, CELLS)
    high = lax.ppermute(low, "dom", down)

    hartree, core, smooth, upper, lower, charge = pl.pallas_call(
        functools.partial(second_kernel, share),
        in_specs=[SMEM] + [VMEM] * 9,
        out_specs=[VMEM] * 6,
        out_shape=[
            f32(EXT, CELLS), f32(CORE, CELLS), f32(CORE, CELLS), f32(24, CELLS), f32(24, CELLS), f32(1, LANES)
        ],
        scratch_shapes=filter_scratch + [field, field, pltpu.VMEM((EXT, CELLS), jnp.float32)],
        compiler_params=LIMIT,
        name="second",
    )(factors, psi, external_potential, core_density, weight, guess_before, guess, guess_after, low, high)

    charge = lax.all_to_all(jnp.broadcast_to(charge[None], (dom_count, 1, LANES)), "dom", 0, 0, tiled=True)
    from_below = lax.ppermute(upper, "dom", up)
    from_above = lax.ppermute(lower, "dom", down)
    charge = charge.sum(axis=0)
    core = jnp.concatenate([core[:8] + from_below[:8], core[8:24], core[24:] + from_above[:8]], axis=0)
    smooth = smooth + jnp.concatenate([from_below[8:], from_above[8:]], axis=0)
    sent = jnp.concatenate(
        [core[:, None], smooth[:, None], jnp.broadcast_to(charge[None], (orb_count, 1, LANES))], axis=2
    )
    arrived = lax.all_to_all(sent, "orb", 0, 0, tiled=True)

    settled = pl.pallas_call(
        decay_kernel,
        in_specs=[VMEM],
        out_specs=VMEM,
        out_shape=f32(CORE, CELLS),
        scratch_shapes=[field, field],
        compiler_params=LIMIT,
        name="decay",
    )(hartree)
    settled = lax.dynamic_slice_in_dim(settled, orb_rank, 1, 0)

    total = arrived.sum(axis=0)
    density = total[:, :CELLS]
    average = total[:, 2 * CELLS : 2 * CELLS + 1] / (dom_count * CORE * CELLS)
    return settled + total[:, CELLS : 2 * CELLS] - (SWEEPS * SOURCE) * average - EXCHANGE_FACTOR * jnp.cbrt(density)


def solution(mesh):
    placed = (
        P("dom", "orb", None, None),
        P("dom", "orb"),
        P("dom"),
        P("dom", None),
        P("dom", None, None),
        P("dom", None, None),
        P(("dom", "orb"), None),
    )
    return jax.shard_map(
        body, mesh=mesh, in_specs=placed, out_specs=P(("dom", "orb"), None), check_vma=False
    )
```

profile of v0, /device:TPU:64, one launch (start us, length us, event | category | flops | bytes accessed | tf_op | source)
XLA Modules:
  0.0 179.8 jit_solution(12703840348546554791)
XLA Ops:
  0.7 0.0 copy-start.8
  0.7 0.6 copy-done.8
  1.3 0.1 copy.24.weight_ref
  1.4 0.0 copy-start.9
  1.4 0.7 copy-done.9
  2.1 0.0 copy-start
  2.1 1.0 copy-done
  3.1 1.0 copy-done.2
  4.1 1.2 copy-done.4
  5.3 16.8 %first.1 = (f32[2,48,2304]{2,1,0:T(8,128)S(1)}, f32[24,2304]{1,0:T(8,128)S(1)}, f32[24,2304]{1,0:T(8,128)S(1)}) custom-call(f32[2]{0:T(128)S(1)} %fusion.4.factor_ref, f32[1,2,48,2304]{3,2,1,0:T(8,128)S(1)} %copy-done.4, f32[1,48,2304]{2,1,0:T(8,128)S(1)} %copy-done, f32[1,48,2304]{2,1,0:T(8,128)S(1)} %copy-done.2, f32[48,1]{1,0:T(8,128)S(1)} %copy.24.weight_ref), custom_call_target="tpu_custom_call" | custom-call | tf_op jit(solution)/shard_map/first/pallas_call | solution.py:282
  22.0 1.9 %collective-permute-start = (f32[24,2304]{1,0:T(8,128)S(1)}, f32[24,2304]{1,0:T(8,128)S(1)}, u32[]{:S(2)}, u32[]{:S(2)}) collective-permute-start(f32[24,2304]{1,0:T(8,128)S(1)} %get-tuple-element.15), channel_id=1, source_target_pairs={{0,32},{32,64},{64,96},{96,128},{128,160},{160,192},{192,224},{224... | collective-permute-start | bytes 663560 | tf_op jit(solution)/shard_map/ppermute | solution.py:292
  24.0 0.0 copy-start.7
  24.0 0.7 copy-done.7
  24.7 6.7 %collective-permute-done = f32[24,2304]{1,0:T(8,128)S(1)} collective-permute-done((f32[24,2304]{1,0:T(8,128)S(1)}, f32[24,2304]{1,0:T(8,128)S(1)}, u32[]{:S(2)}, u32[]{:S(2)}) %collective-permute-start) | collective-permute-done | bytes 221216 | tf_op jit(solution)/shard_map/ppermute | solution.py:292
  31.5 0.6 copy.25
  32.1 32.1 %all_to_all.20 = f32[32,1,4608]{2,1,0:T(1,128)S(1)} all-to-all(f32[32,1,4608]{2,1,0:T(1,128)S(1)} %copy.25), channel_id=1, replica_groups=mesh['dom'=16,'orb'=32] {'orb'}, dimensions={0} | all-to-all | bytes 1179648 | tf_op jit(solution)/shard_map/all_to_all | solution.py:297
  64.3 0.2 slice_reduce_fusion
  64.4 0.2 broadcast_in_dim.45
  64.6 19.0 %all_to_all.21 = f32[32,1,2304]{2,1,0:T(1,128)S(1)} all-to-all(f32[32,1,2304]{2,1,0:T(1,128)S(1)} %broadcast_in_dim.45), channel_id=1, replica_groups=mesh['dom'=16,'orb'=32] {'orb'}, dimensions={0} | all-to-all | bytes 589824 | tf_op jit(solution)/shard_map/all_to_all | solution.py:302
  83.7 4.8 %collective-permute-start.3 = (f32[32,2304]{1,0:T(8,128)S(1)}, f32[32,2304]{1,0:T(8,128)S(1)}, u32[]{:S(2)}, u32[]{:S(2)}) collective-permute-start(f32[32,2304]{1,0:T(8,128)S(1)} %bitcast.26), channel_id=1, source_target_pairs={{32,0},{64,32},{96,64},{128,96},{160,128},{192,160},{224,192},{256... | collective-permute-start | bytes 884744 | tf_op jit(solution)/shard_map/ppermute | solution.py:304
  88.6 0.0 copy-start.1
  88.6 0.0 copy-start.3
  88.6 2.1 %collective-permute-start.1 = (f32[16,2304]{1,0:T(8,128)S(1)}, f32[16,2304]{1,0:T(8,128)S(1)}, u32[]{:S(2)}, u32[]{:S(2)}) collective-permute-start(f32[16,2304]{1,0:T(8,128)S(1)} %bitcast.31), channel_id=1, source_target_pairs={{0,32},{32,64},{64,96},{96,128},{128,160},{160,192},{192,224},{224... | collective-permute-start | bytes 442376 | tf_op jit(solution)/shard_map/ppermute | solution.py:300
  90.7 5.8 %collective-permute-start.2 = (f32[16,2304]{1,0:T(8,128)S(1)}, f32[16,2304]{1,0:T(8,128)S(1)}, u32[]{:S(2)}, u32[]{:S(2)}) collective-permute-start(f32[16,2304]{1,0:T(8,128)S(1)} %bitcast.30), channel_id=1, source_target_pairs={{32,0},{64,32},{96,64},{128,96},{160,128},{192,160},{224,192},{256... | collective-permute-start | bytes 442376 | tf_op jit(solution)/shard_map/ppermute | solution.py:301
  96.4 0.9 collective-permute-done.1.before_ref
  97.3 1.8 collective-permute-done.2.after_ref
  99.1 0.0 collective-permute-done.3.high_ref
  99.1 0.0 copy-done.1
  99.1 0.0 copy-done.3
  99.1 28.4 %second.1 = (f32[64,2304]{1,0:T(8,128)S(1)}, f32[32,2304]{1,0:T(8,128)S(1)}, f32[32,2304]{1,0:T(8,128)S(1)}, f32[24,2304]{1,0:T(8,128)S(1)}, f32[24,2304]{1,0:T(8,128)S(1)}, /*index=5*/f32[1,128]{1,0:T(1,128)S(1)}) custom-call(f32[2]{0:T(128)S(1)} %fusion.4.factor_ref, f32[2,48,2304]{2,1,0:T(8,128)S(1)} %get-tuple-element.14.psi_ref, ...), custom_call_target="tpu_custom_call" | custom-call | tf_op jit(solution)/shard_map/second/pallas_call | solution.py:306
  127.5 1.9 %collective-permute-start.4 = (f32[24,2304]{1,0:T(8,128)S(1)}, f32[24,2304]{1,0:T(8,128)S(1)}, u32[]{:S(2)}, u32[]{:S(2)}) collective-permute-start(f32[24,2304]{1,0:T(8,128)S(1)} %get-tuple-element.19), channel_id=1, source_target_pairs={{0,32},{32,64},{64,96},{96,128},{128,160},{160,192},{192,224},{224... | collective-permute-start | bytes 663560 | tf_op jit(solution)/shard_map/ppermute | solution.py:319
  129.4 5.9 %collective-permute-start.5 = (f32[24,2304]{1,0:T(8,128)S(1)}, f32[24,2304]{1,0:T(8,128)S(1)}, u32[]{:S(2)}, u32[]{:S(2)}) collective-permute-start(f32[24,2304]{1,0:T(8,128)S(1)} %get-tuple-element.20), channel_id=1, source_target_pairs={{32,0},{64,32},{96,64},{128,96},{160,128},{192,160},{224,192},{256... | collective-permute-start | bytes 663560 | tf_op jit(solution)/shard_map/ppermute | solution.py:320
  135.3 0.6 broadcast_in_dim.49
  136.0 3.5 %all-to-all-start.2 = ((f32[16,1,128]{2,1,0:T(1,128)}), f32[16,1,128]{2,1,0:T(1,128)S(1)}, u32[]{:S(2)}, u32[]{:S(2)}) async-start(f32[16,1,128]{2,1,0:T(1,128)} %broadcast_in_dim.49), calls=%async_computation.2 | async-start | bytes 16384 | tf_op jit(solution)/shard_map/all_to_all | solution.py:318
  139.4 5.9 %all-to-all-done.2 = f32[16,1,128]{2,1,0:T(1,128)S(1)} async-done(((f32[16,1,128]{2,1,0:T(1,128)}), f32[16,1,128]{2,1,0:T(1,128)S(1)}, u32[]{:S(2)}, u32[]{:S(2)}) %all-to-all-start.2) | async-done | bytes 8224 | tf_op jit(solution)/shard_map/all_to_all | solution.py:318
  145.4 0.0 collective-permute-done.4
  145.4 0.0 copy-start.5
  145.4 0.7 copy-done.5
  146.1 0.0 collective-permute-done.5
  146.1 0.9 slice-done
  147.0 0.9 copy-done.6
  148.0 1.4 copy.31
  149.5 6.0 %all-to-all-start.3 = ((f32[32,1,4736]{2,1,0:T(1,128)}), f32[32,1,4736]{2,1,0:T(1,128)S(1)}, u32[]{:S(2)}, u32[]{:S(2)}) async-start(f32[32,1,4736]{2,1,0:T(1,128)} %copy.31), calls=%async_computation.3 | async-start | bytes 1212416 | tf_op jit(solution)/shard_map/all_to_all | solution.py:327
  155.4 6.4 %decay.1 = f32[32,2304]{1,0:T(8,128)S(1)} custom-call(f32[64,2304]{1,0:T(8,128)S(1)} %get-tuple-element.17.hartree_ref), custom_call_target="tpu_custom_call" | custom-call | tf_op jit(solution)/shard_map/decay/pallas_call | solution.py:329
  161.9 15.7 %all-to-all-done.3 = f32[32,1,4736]{2,1,0:T(1,128)S(1)} async-done(((f32[32,1,4736]{2,1,0:T(1,128)}), f32[32,1,4736]{2,1,0:T(1,128)S(1)}, u32[]{:S(2)}, u32[]{:S(2)}) %all-to-all-start.3) | async-done | bytes 606240 | tf_op jit(solution)/shard_map/all_to_all | solution.py:327
  177.6 0.3 reduce_sum.31
  177.9 0.5 slice.93
  179.1 0.7 fusion.2
  (26 shorter events, 0.4 us)
Async XLA Ops:
  0.7 0.7 copy-start.8
  1.4 0.7 copy-start.9
  2.1 1.0 copy-start
  3.1 1.0 copy-start.2
  4.1 1.2 copy-start.4
  22.0 9.4 %collective-permute-start = (f32[24,2304]{1,0:T(8,128)S(1)}, f32[24,2304]{1,0:T(8,128)S(1)}, u32[]{:S(2)}, u32[]{:S(2)}) collective-permute-start(f32[24,2304]{1,0:T(8,128)S(1)} %get-tuple-element.15), channel_id=1, source_target_pairs={{0,32},{32,64},{64,96},{96,128},{128,160},{160,192},{192,224},{224... | collective-permute-start | bytes 663560 | tf_op jit(solution)/shard_map/ppermute | solution.py:292
  24.0 0.7 copy-start.7
  83.7 15.4 %collective-permute-start.3 = (f32[32,2304]{1,0:T(8,128)S(1)}, f32[32,2304]{1,0:T(8,128)S(1)}, u32[]{:S(2)}, u32[]{:S(2)}) collective-permute-start(f32[32,2304]{1,0:T(8,128)S(1)} %bitcast.26), channel_id=1, source_target_pairs={{32,0},{64,32},{96,64},{128,96},{160,128},{192,160},{224,192},{256... | collective-permute-start | bytes 884744 | tf_op jit(solution)/shard_map/ppermute | solution.py:304
  88.6 10.5 %copy-start.1 = (f32[1,48,2304]{2,1,0:T(8,128)S(1)}, f32[1,48,2304]{2,1,0:T(8,128)}, u32[]{:S(2)}) copy-start(f32[1,48,2304]{2,1,0:T(8,128)} %ext_ref.3) | copy-start | bytes 1327108
  88.6 10.5 %copy-start.3 = (f32[1,48,2304]{2,1,0:T(8,128)S(1)}, f32[1,48,2304]{2,1,0:T(8,128)}, u32[]{:S(2)}) copy-start(f32[1,48,2304]{2,1,0:T(8,128)} %core_ref.3) | copy-start | bytes 1327108
  88.6 8.7 %collective-permute-start.1 = (f32[16,2304]{1,0:T(8,128)S(1)}, f32[16,2304]{1,0:T(8,128)S(1)}, u32[]{:S(2)}, u32[]{:S(2)}) collective-permute-start(f32[16,2304]{1,0:T(8,128)S(1)} %bitcast.31), channel_id=1, source_target_pairs={{0,32},{32,64},{64,96},{96,128},{128,160},{160,192},{192,224},{224... | collective-permute-start | bytes 442376 | tf_op jit(solution)/shard_map/ppermute | solution.py:300
  90.7 8.4 %collective-permute-start.2 = (f32[16,2304]{1,0:T(8,128)S(1)}, f32[16,2304]{1,0:T(8,128)S(1)}, u32[]{:S(2)}, u32[]{:S(2)}) collective-permute-start(f32[16,2304]{1,0:T(8,128)S(1)} %bitcast.30), channel_id=1, source_target_pairs={{32,0},{64,32},{96,64},{128,96},{160,128},{192,160},{224,192},{256... | collective-permute-start | bytes 442376 | tf_op jit(solution)/shard_map/ppermute | solution.py:301
  127.5 17.9 %collective-permute-start.4 = (f32[24,2304]{1,0:T(8,128)S(1)}, f32[24,2304]{1,0:T(8,128)S(1)}, u32[]{:S(2)}, u32[]{:S(2)}) collective-permute-start(f32[24,2304]{1,0:T(8,128)S(1)} %get-tuple-element.19), channel_id=1, source_target_pairs={{0,32},{32,64},{64,96},{96,128},{128,160},{160,192},{192,224},{224... | collective-permute-start | bytes 663560 | tf_op jit(solution)/shard_map/ppermute | solution.py:319
  129.4 16.6 %collective-permute-start.5 = (f32[24,2304]{1,0:T(8,128)S(1)}, f32[24,2304]{1,0:T(8,128)S(1)}, u32[]{:S(2)}, u32[]{:S(2)}) collective-permute-start(f32[24,2304]{1,0:T(8,128)S(1)} %get-tuple-element.20), channel_id=1, source_target_pairs={{32,0},{64,32},{96,64},{128,96},{160,128},{192,160},{224,192},{256... | collective-permute-start | bytes 663560 | tf_op jit(solution)/shard_map/ppermute | solution.py:320
  136.0 9.4 %all-to-all-start.2 = ((f32[16,1,128]{2,1,0:T(1,128)}), f32[16,1,128]{2,1,0:T(1,128)S(1)}, u32[]{:S(2)}, u32[]{:S(2)}) async-start(f32[16,1,128]{2,1,0:T(1,128)} %broadcast_in_dim.49), calls=%async_computation.2 | async-start | bytes 16384 | tf_op jit(solution)/shard_map/all_to_all | solution.py:318
  145.4 0.7 copy-start.5
  146.1 0.9 slice-start
  147.0 0.9 copy-start.6
  149.5 28.1 %all-to-all-start.3 = ((f32[32,1,4736]{2,1,0:T(1,128)}), f32[32,1,4736]{2,1,0:T(1,128)S(1)}, u32[]{:S(2)}, u32[]{:S(2)}) async-start(f32[32,1,4736]{2,1,0:T(1,128)} %copy.31), calls=%async_computation.3 | async-start | bytes 1212416 | tf_op jit(solution)/shard_map/all_to_all | solution.py:327
where the time goes:
time: 181 us; the launch traced here: 180 us
  Pallas kernels  51.6 us (29%)
  blocking collectives  51.2 us (28%)
  starting transfers between devices  31.8 us (18%)
  waiting for transfers between devices  30.9 us (17%)
  local copies, waits for them, and re-layouts  11.2 us (6%)
    all_to_all x1, blocking collectives, body(): arrived = lax.all_to_all(sent, 'orb', 0, 0, tiled=True)  32.1 us
    pallas_call x1, Pallas kernels, body(): pl.pallas_call(functools.partial(second_kernel, share), in_specs=[SMEM] +...  28.4 us
    all_to_all x1, blocking collectives, body(): lax.all_to_all(jnp.broadcast_to(plane[None], (orb_count, 1, CELLS)), 'orb...  19 us
    pallas_call x1, Pallas kernels, body(): pl.pallas_call(functools.partial(first_kernel, share), in_specs=[SMEM] +...  16.8 us
    all_to_all x1, waiting for transfers between devices, body(): arrived = lax.all_to_all(sent, 'orb', 0, 0, tiled=True)  15.7 us
    unnamed x24, local copies, waits for them, and re-layouts  6.82 us
    ppermute x1, waiting for transfers between devices, body(): behind = lax.ppermute(upper, 'dom', up)  6.69 us
    pallas_call x1, Pallas kernels, body(): pl.pallas_call(decay_kernel, in_specs=[VMEM], out_specs=VMEM, out_shape=f...  6.45 us
  transfers between devices with their start and end apart: 8, of which 5 were waited for; matrix products, arithmetic and copies ran while one was open for 0% of the time, Pallas kernels for 4%

commit v1 on v0

v1 whole, which is shorter than its diff:
```python
import functools

import jax
import jax.numpy as jnp
from jax import lax
from jax.experimental import pallas as pl
from jax.experimental.pallas import tpu as pltpu
from jax.sharding import PartitionSpec as P

SIDE = 48
CORE = 32
BUF = 8
DEGREE = 8
SWEEPS = 4
BOX = 48
CELLS = SIDE * SIDE
LANES = 128
COLS = CELLS // LANES
PAD = 8
EXT = 64
SHIFT = 12
UP = 20
BLOCK = 384
BLOCKS = CELLS // BLOCK
DEPTH = BLOCK + LANES
TILE = 16

EXCHANGE_FACTOR = (3.0 / 3.141592653589793) ** (1.0 / 3.0)
FOUR_PI = 4.0 * 3.141592653589793
RELAXATION = 0.8
CUTOFF = 1.5
KEEP = 1.0 - RELAXATION
SPREAD = RELAXATION / 6.0
SOURCE = SPREAD * FOUR_PI


def build_neighbours(matrix_ref):
    rows = lax.broadcasted_iota(jnp.int32, (DEPTH, BLOCK), 0)
    cols = lax.broadcasted_iota(jnp.int32, (DEPTH, BLOCK), 1)
    edge = rows - BLOCK
    inside = rows < BLOCK
    after = edge < SIDE
    before = edge >= LANES - SIDE
    row_y = jnp.where(inside, rows // SIDE, jnp.where(after, SIDE // 6, jnp.where(before, -1, -9)))
    row_x = jnp.where(inside, rows % SIDE, jnp.where(after, edge, edge - (LANES - SIDE)))
    col_y = cols // SIDE
    col_x = cols % SIDE
    gap_x = jnp.abs(row_x - col_x)
    along = (row_y == col_y) & ((gap_x == 1) | (gap_x == SIDE - 1))
    across = (row_x == col_x) & (jnp.abs(row_y - col_y) == 1)
    ones = jnp.where(along | across, 1.0, 0.0).astype(jnp.bfloat16)
    matrix_ref[0:DEPTH, :] = ones
    matrix_ref[DEPTH : 2 * DEPTH, :] = ones


def tile_of(ref, start):
    return [ref[pl.ds(start, 8), pl.ds(LANES * i, LANES)] for i in range(COLS)]


def put_tile(ref, start, pieces):
    for i in range(COLS):
        ref[pl.ds(start, 8), pl.ds(LANES * i, LANES)] = pieces[i]


def put_split(split_ref, planes, start, upper, lower):
    lane = lax.broadcasted_iota(jnp.int32, (TILE, LANES), 1)
    both = [jnp.concatenate([upper[i], lower[i]], axis=0) for i in range(COLS)]
    high = [x.astype(jnp.bfloat16) for x in both]
    low = [(both[i] - high[i].astype(jnp.float32)).astype(jnp.bfloat16) for i in range(COLS)]
    for b in range(BLOCKS):
        rows = pl.ds(b * planes + start, TILE)
        for k, half in enumerate((high, low)):
            base = k * DEPTH
            for j in range(3):
                split_ref[rows, pl.ds(base + LANES * j, LANES)] = half[3 * b + j]
            edge = jnp.where(lane < SIDE, half[(3 * b + 3) % COLS], half[(3 * b - 1) % COLS])
            split_ref[rows, pl.ds(base + BLOCK, LANES)] = edge


def multiply(split_ref, matrix_ref, sum_ref, rows):
    sum_ref[0:rows, :] = jnp.dot(
        split_ref[0:rows, :], matrix_ref[...], preferred_element_type=jnp.float32
    )


def sum_tile(sum_ref, planes, start):
    return [
        sum_ref[pl.ds((i // 3) * planes + start, 8), pl.ds(LANES * (i % 3), LANES)] for i in range(COLS)
    ]


def around(flat, before, here, after):
    row = lax.broadcasted_iota(jnp.int32, (8, LANES), 0)
    out = []
    for i in range(COLS):
        lower = pltpu.roll(jnp.where(row == 7, before[i], here[i]), 1, 0)
        upper = pltpu.roll(jnp.where(row == 0, after[i], here[i]), 7, 0)
        out.append(flat[i] + (lower + upper))
    return out


def clear_pads(refs, planes):
    zero = jnp.zeros((PAD, CELLS), jnp.float32)
    for ref in refs:
        ref[0:PAD, :] = zero
        ref[PAD + planes : 2 * PAD + planes, :] = zero


def split_all(source, split_ref, planes):
    for s in range(0, planes, TILE):
        put_split(split_ref, planes, s, tile_of(source, PAD + s), tile_of(source, PAD + s + 8))


def update(source, target, split_ref, sum_ref, planes, rule):
    for s in range(0, planes, TILE):
        tiles = [tile_of(source, PAD + s + 8 * k) for k in range(-1, 3)]
        new = []
        for k in range(2):
            total = around(sum_tile(sum_ref, planes, s + 8 * k), *tiles[k : k + 3])
            new.append(rule(s + 8 * k, tiles[k + 1], total))
            put_tile(target, PAD + s + 8 * k, new[k])
        if split_ref is not None:
            put_split(split_ref, planes, s, *new)


def scaled_potential(v_tile, w_ref):
    low = high = None
    for t in range(BOX // 8):
        for v in v_tile(8 * t):
            low = v if low is None else jnp.minimum(low, v)
            high = v if high is None else jnp.maximum(high, v)
    low = jnp.min(low, keepdims=True) + CUTOFF
    high = jnp.max(high, keepdims=True) + 6.0
    center = 0.5 * (high + low)
    inverse = 1.0 / (0.5 * (high - low))
    offset = jnp.broadcast_to((3.0 - center) * (2.0 * inverse), (8, LANES))
    double = jnp.broadcast_to(2.0 * inverse, (8, LANES))
    for t in range(BOX // 8):
        put_tile(w_ref, 8 * t, [double * v + offset for v in v_tile(8 * t)])
    return jnp.broadcast_to(inverse, (8, LANES))


def run_filter(a_refs, b_refs, splits, sums, matrix_ref, w_ref, single):
    orbs = len(a_refs)

    def first_rule(q):
        def rule(r, here, total):
            w = tile_of(w_ref, r)
            return [0.5 * (w[i] * here[i] - single * total[i]) for i in range(COLS)]

        return rule

    def next_rule(q, target):
        def rule(r, here, total):
            w = tile_of(w_ref, r)
            old = tile_of(target[q], PAD + r)
            return [(w[i] * here[i] - single * total[i]) - old[i] for i in range(COLS)]

        return rule

    def step(source, target, rules, last=False):
        for q in range(orbs):
            multiply(splits[q], matrix_ref, sums[q], BLOCKS * BOX)
        for q in range(orbs):
            update(source[q], target[q], None if last else splits[q], sums[q], BOX, rules(q))

    for q in range(orbs):
        split_all(a_refs[q], splits[q], BOX)
    step(a_refs, b_refs, first_rule)

    def pair(k, carry):
        step(b_refs, a_refs, lambda q: next_rule(q, a_refs))
        step(a_refs, b_refs, lambda q: next_rule(q, b_refs))
        return carry

    lax.fori_loop(0, (DEGREE - 2) // 2, pair, 0)
    step(b_refs, a_refs, lambda q: next_rule(q, a_refs), last=True)


def norms(a_refs):
    out = []
    for ref in a_refs:
        total = [jnp.zeros((8, LANES), jnp.float32) for _ in range(3)]
        for t in range(BOX // 8):
            for i, y in enumerate(tile_of(ref, PAD + 8 * t)):
                total[i % 3] = total[i % 3] + y * y
        mean = jnp.sum(total[0] + total[1] + total[2], keepdims=True) * (1.0 / (BOX * CELLS))
        out.append(jnp.broadcast_to(lax.rsqrt(mean + 1e-06), (8, LANES)))
    return out


def density_tile(a_refs, scale, factor_ref, core_ref, weight_ref, t, share, psi_out):
    weight = jnp.broadcast_to(weight_ref[8 * t : 8 * t + 8, :], (8, LANES))
    total = [share * c for c in tile_of(core_ref, 8 * t)]
    for q, ref in enumerate(a_refs):
        y = [p * scale[q] for p in tile_of(ref, PAD + 8 * t)]
        if psi_out is not None:
            put_tile(psi_out.at[q], 8 * t, y)
        total = [total[i] + factor_ref[q] * (y[i] * y[i]) for i in range(COLS)]
    return [weight * d for d in total]


def relax(plane_ref, row, g_ref, h_ref, d_ref, split_ref, sum_ref, matrix_ref):
    clear_pads((g_ref, h_ref), EXT)
    g_ref[PAD : PAD + EXT, :] = jnp.zeros((EXT, CELLS), jnp.float32)
    g_ref[pl.ds(PAD + row, 1), :] = plane_ref[...]

    def rule(r, here, total):
        push = tile_of(d_ref, r)
        return [KEEP * here[i] + SPREAD * total[i] + SOURCE * push[i] for i in range(COLS)]

    def one(source, target, last=False):
        multiply(split_ref, matrix_ref, sum_ref, BLOCKS * EXT)
        update(source, target, None if last else split_ref, sum_ref, EXT, rule)

    split_all(g_ref, split_ref, EXT)
    for k in range(SWEEPS // 2):
        one(g_ref, h_ref)
        one(h_ref, g_ref, last=k == SWEEPS // 2 - 1)


def first_kernel(
    share, factor_ref, rank_ref, orbitals_ref, ext_ref, core_ref, weight_ref, guess_ref,
    psi_out, frame_out, smooth_out, up_out,
    a0, a1, b0, b1, x0, x1, s0, s1, w_ref, g_ref, h_ref, d_ref, matrix_ref, v_ref, c_ref, sem,
):
    copies = [
        pltpu.make_async_copy(ext_ref.at[0], v_ref, sem.at[0]),
        pltpu.make_async_copy(orbitals_ref.at[0, 0], a0.at[PAD : PAD + BOX], sem.at[1]),
        pltpu.make_async_copy(orbitals_ref.at[0, 1], a1.at[PAD : PAD + BOX], sem.at[2]),
        pltpu.make_async_copy(core_ref.at[0], c_ref, sem.at[3]),
    ]
    for copy in copies:
        copy.start()
    build_neighbours(matrix_ref)
    clear_pads((a0, a1, b0, b1), BOX)
    copies[0].wait()
    single = scaled_potential(lambda r: tile_of(v_ref, r), w_ref)
    copies[1].wait()
    copies[2].wait()
    run_filter((a0, a1), (b0, b1), (x0, x1), (s0, s1), matrix_ref, w_ref, single)
    scale = norms((a0, a1))
    copies[3].wait()
    zero = jnp.zeros((8, CELLS), jnp.float32)
    d_ref[0:8, :] = zero
    d_ref[56:64, :] = zero
    for t in range(BOX // 8):
        put_tile(d_ref, 8 + 8 * t, density_tile((a0, a1), scale, factor_ref, c_ref, weight_ref, t, share, psi_out))
    relax(guess_ref, 16 + rank_ref[0], g_ref, h_ref, d_ref, x0, s0, matrix_ref)
    low = 16 - SHIFT
    frame_out[...] = d_ref[low : low + CORE, :]
    smooth_out[...] = g_ref[PAD + low : PAD + low + CORE, :]
    up_out[0:UP, :] = d_ref[low + CORE : low + CORE + UP, :]
    up_out[UP : 48, :] = g_ref[PAD + low + CORE : PAD + EXT, :]


def second_kernel(
    share, factor_ref, rank_ref, psi_ref, ext_ref, core_ref, weight_ref, plane_ref, low_ref, high_ref,
    core_out, smooth_out, up_out, down_out, charge_out,
    a0, a1, b0, b1, x0, x1, s0, s1, w_ref, g_ref, h_ref, d_ref, matrix_ref,
):
    build_neighbours(matrix_ref)
    clear_pads((a0, a1, b0, b1), BOX)
    a0[PAD : PAD + BOX, :] = psi_ref[0]
    a1[PAD : PAD + BOX, :] = psi_ref[1]
    first = SHIFT - BUF
    h_ref[0 : CORE - first, :] = low_ref[first:CORE, :]
    h_ref[CORE - first : BOX, :] = high_ref[...]
    for t in range(BOX // 8):
        ionic = tile_of(ext_ref, 8 * t)
        own = tile_of(h_ref, 8 * t)
        put_tile(h_ref, 8 * t, [ionic[i] + own[i] for i in range(COLS)])
    single = scaled_potential(lambda r: tile_of(h_ref, r), w_ref)
    run_filter((a0, a1), (b0, b1), (x0, x1), (s0, s1), matrix_ref, w_ref, single)
    scale = norms((a0, a1))
    zero = jnp.zeros((8, CELLS), jnp.float32)
    d_ref[0:8, :] = zero
    d_ref[56:64, :] = zero
    charge = [jnp.zeros((8, LANES), jnp.float32) for _ in range(3)]
    for t in range(BOX // 8):
        tile = density_tile((a0, a1), scale, factor_ref, core_ref, weight_ref, t, share, None)
        put_tile(d_ref, 8 + 8 * t, tile)
        for i, d in enumerate(tile):
            charge[i % 3] = charge[i % 3] + d
    charge_out[...] = jnp.broadcast_to(jnp.sum(charge[0] + charge[1] + charge[2], keepdims=True), charge_out.shape)
    relax(plane_ref, 16 - SHIFT + rank_ref[0], g_ref, h_ref, d_ref, x0, s0, matrix_ref)
    core_out[...] = d_ref[16:48, :]
    down_out[0:8, :] = d_ref[8:16, :]
    up_out[0:8, :] = d_ref[48:56, :]
    down_out[8:24, :] = g_ref[PAD : PAD + 16, :]
    smooth_out[...] = g_ref[PAD + 16 : PAD + 48, :]
    up_out[8:24, :] = g_ref[PAD + 48 : PAD + 64, :]


VMEM = pl.BlockSpec(memory_space=pltpu.VMEM)
SMEM = pl.BlockSpec(memory_space=pltpu.SMEM)
ANY = pl.BlockSpec(memory_space=pl.ANY)
LIMIT = pltpu.CompilerParams(vmem_limit_bytes=48 * 2**20)


def f32(*shape):
    return jax.ShapeDtypeStruct(shape, jnp.float32)


def body(orbitals, occupations, occupied_count, weights, external_potential, core_density, hartree_guess):
    orb_count = lax.axis_size("orb")
    dom_count = lax.axis_size("dom")
    orb_rank = lax.axis_index("orb")
    per_device = orbitals.shape[1]
    rank = orb_rank * per_device + jnp.arange(per_device, dtype=jnp.int32)
    factors = jnp.where(rank < occupied_count[0], occupations[0], jnp.float32(0.0)) / (per_device * orb_count)
    weight = weights.reshape(BOX, 1)
    place = orb_rank.reshape(1)
    share = 1.0 / orb_count
    up = [(i, (i + 1) % dom_count) for i in range(dom_count)]
    down = [(j, i) for i, j in up]
    padded = pltpu.VMEM((BOX + 2 * PAD, CELLS), jnp.float32)
    wide = pltpu.VMEM((EXT + 2 * PAD, CELLS), jnp.float32)
    split = pltpu.VMEM((BLOCKS * EXT, 2 * DEPTH), jnp.bfloat16)
    sums = pltpu.VMEM((BLOCKS * EXT, BLOCK), jnp.float32)
    box = pltpu.VMEM((BOX, CELLS), jnp.float32)
    scratch = [padded] * 4 + [split] * 2 + [sums] * 2 + [
        box, wide, wide, pltpu.VMEM((EXT, CELLS), jnp.float32), pltpu.VMEM((2 * DEPTH, BLOCK), jnp.bfloat16)
    ]

    psi, frame, smooth, upper = pl.pallas_call(
        functools.partial(first_kernel, share),
        in_specs=[SMEM] * 2 + [ANY] * 3 + [VMEM] * 2,
        out_specs=[VMEM] * 4,
        out_shape=[f32(per_device, BOX, CELLS), f32(CORE, CELLS), f32(CORE, CELLS), f32(48, CELLS)],
        scratch_shapes=scratch + [box, box, pltpu.SemaphoreType.DMA((4,))],
        compiler_params=LIMIT,
        name="first",
    )(factors, place, orbitals, external_potential, core_density, weight, hartree_guess)

    behind = lax.ppermute(upper, "dom", up)
    frame = jnp.concatenate([frame[:UP] + behind[:UP], frame[UP:]], axis=0)
    smooth = jnp.concatenate([smooth[:28] + behind[UP:], smooth[28:]], axis=0)
    sent = jnp.concatenate([frame[:, None], smooth[:, None]], axis=2)
    arrived = lax.all_to_all(sent, "orb", 0, 0, tiled=True)
    total = arrived.sum(axis=0)
    owned_density = total[:, :CELLS]
    owned_hartree = total[:, CELLS:]
    plane = owned_hartree - EXCHANGE_FACTOR * jnp.cbrt(owned_density)
    low = lax.all_to_all(jnp.broadcast_to(plane[None], (orb_count, 1, CELLS)), "orb", 0, 0, tiled=True)
    low = low.reshape(CORE, CELLS)
    high = lax.ppermute(low[:UP], "dom", down)

    core, smooth, upper, lower, charge = pl.pallas_call(
        functools.partial(second_kernel, share),
        in_specs=[SMEM] * 2 + [VMEM] * 7,
        out_specs=[VMEM] * 5,
        out_shape=[f32(CORE, CELLS), f32(CORE, CELLS), f32(24, CELLS), f32(24, CELLS), f32(1, LANES)],
        scratch_shapes=scratch,
        compiler_params=LIMIT,
        name="second",
    )(factors, place, psi, external_potential[0], core_density[0], weight, owned_hartree, low, high)

    charge = charge + jnp.sum(owned_density)
    charge = lax.all_to_all(jnp.broadcast_to(charge[None], (dom_count, 1, LANES)), "dom", 0, 0, tiled=True)
    from_below = lax.ppermute(upper, "dom", up)
    from_above = lax.ppermute(lower, "dom", down)
    charge = charge.sum(axis=0)
    core = jnp.concatenate([core[:8] + from_below[:8], core[8:24], core[24:] + from_above[:8]], axis=0)
    smooth = smooth + jnp.concatenate([from_below[8:], from_above[8:]], axis=0)
    sent = jnp.concatenate(
        [core[:, None], smooth[:, None], jnp.broadcast_to(charge[None], (orb_count, 1, LANES))], axis=2
    )
    arrived = lax.all_to_all(sent, "orb", 0, 0, tiled=True)
    total = arrived.sum(axis=0)
    density = total[:, :CELLS]
    average = total[:, 2 * CELLS : 2 * CELLS + 1] / (dom_count * CORE * CELLS)
    return total[:, CELLS : 2 * CELLS] - (SWEEPS * SOURCE) * average - EXCHANGE_FACTOR * jnp.cbrt(density)


def solution(mesh):
    placed = (
        P("dom", "orb", None, None),
        P("dom", "orb"),
        P("dom"),
        P("dom", None),
        P("dom", None, None),
        P("dom", None, None),
        P(("dom", "orb"), None),
    )
    return jax.shard_map(
        body, mesh=mesh, in_specs=placed, out_specs=P(("dom", "orb"), None), check_vma=False
    )
```

time: 181 us -> 153 us (0.85)
  Pallas kernels: 51.6 us -> 22.8 us
  blocking collectives: 51.2 us -> 79 us
  starting transfers between devices: 31.8 us -> 18.4 us
  waiting for transfers between devices: 30.9 us -> 18.9 us
  local copies, waits for them, and re-layouts: 11.2 us -> 8.75 us
    pallas_call x3 -> x2, Pallas kernels: 51.6 us -> 22.8 us  [the longest x1 12.2 us: body(): pl.pallas_call(functools.partial(first_kernel, share), in_specs=[SMEM] *...]
    all_to_all x1 -> x2, blocking collectives: 32.1 us -> 60 us  [body(): arrived = lax.all_to_all(sent, 'orb', 0, 0, tiled=True)]
    all_to_all x1 -> x0, waiting for transfers between devices: 15.7 us -> none  [body(): arrived = lax.all_to_all(sent, 'orb', 0, 0, tiled=True)]
    ppermute x3 -> x1, starting transfers between devices: 12.6 us -> 5.13 us  [body(): high = lax.ppermute(low[:UP], 'dom', down)]
    all_to_all x1 -> x0, starting transfers between devices: 5.96 us -> none  [body(): arrived = lax.all_to_all(sent, 'orb', 0, 0, tiled=True)]
    ppermute x1, waiting for transfers between devices: 6.69 us -> 9.76 us  [body(): behind = lax.ppermute(upper, 'dom', up)]
    unnamed x24 -> x20, local copies, waits for them, and re-layouts: 6.82 us -> 5.16 us
  transfers between devices with their start and end apart: 8 -> 5, of which waited for: 5 -> 3; matrix products, arithmetic and copies ran while one was open for 0% -> 1% of each run, Pallas kernels for 4% -> 0%
where the time goes in v1:
time: 153 us; the launch traced here: 152 us
  blocking collectives  79 us (52%)
  Pallas kernels  22.8 us (15%)
  waiting for transfers between devices  18.9 us (12%)
  starting transfers between devices  18.4 us (12%)
  local copies, waits for them, and re-layouts  8.75 us (6%)
  other arithmetic  3.01 us (2%)
  between operations  1.56 us (1%)
    all_to_all x2, blocking collectives, body(): arrived = lax.all_to_all(sent, 'orb', 0, 0, tiled=True)  60 us
    all_to_all x1, blocking collectives, body(): lax.all_to_all(jnp.broadcast_to(plane[None], (orb_count, 1, CELLS)), 'orb...  19.1 us
    pallas_call x1, Pallas kernels, body(): pl.pallas_call(functools.partial(first_kernel, share), in_specs=[SMEM] *...  12.2 us
    pallas_call x1, Pallas kernels, body(): pl.pallas_call(functools.partial(second_kernel, share), in_specs=[SMEM] *...  10.6 us
    ppermute x1, waiting for transfers between devices, body(): behind = lax.ppermute(upper, 'dom', up)  9.76 us
    ppermute x1, starting transfers between devices, body(): from_above = lax.ppermute(lower, 'dom', down)  5.92 us
    all_to_all x1, waiting for transfers between devices, body(): lax.all_to_all(jnp.broadcast_to(charge[None], (dom_count, 1, LANES)), 'do...  5.89 us
    unnamed x20, local copies, waits for them, and re-layouts  5.16 us
  transfers between devices with their start and end apart: 5, of which 3 were waited for; matrix products, arithmetic and copies ran while one was open for 1% of the time, Pallas kernels for 0%

profile of v1, /device:TPU:64, one launch (start us, length us, event | category | flops | bytes accessed | tf_op | source)
XLA Modules:
  0.0 152.4 jit_solution(2806413887931614776)
XLA Ops:
  0.7 0.0 copy-start.7
  0.7 0.6 copy-done.7
  1.3 0.0 copy-start.5
  1.3 0.1 copy.20.weight_ref
  1.4 0.0 copy-start.8
  1.4 0.7 copy-done.8
  2.1 0.0 copy-done.5
  2.1 0.0 copy-start
  2.1 1.0 copy-done
  3.1 0.0 copy-start.2
  3.1 1.0 copy-done.2
  4.1 0.0 copy-start.4
  4.1 1.2 copy-done.4
  5.3 12.2 %first.1 = (f32[2,48,2304]{2,1,0:T(8,128)S(1)}, f32[32,2304]{1,0:T(8,128)S(1)}, f32[32,2304]{1,0:T(8,128)S(1)}, f32[48,2304]{1,0:T(8,128)S(1)}) custom-call(f32[2]{0:T(128)S(1)} %fusion.3.factor_ref, s32[1]{0:T(128)} %bitcast.2.rank_ref, f32[1,2,48,2304]{3,2,1,0:T(8,128)S(1)} %copy-done.4, f32[1,48,2304]{2,1,0:T(8,128)S(1)} %copy-done, ...), custom_call_target="tpu_custom_call" | custom-call | tf_op jit(solution)/shard_map/first/pallas_call | solution.py:326
  17.5 1.9 %collective-permute-start = (f32[48,2304]{1,0:T(8,128)S(1)}, f32[48,2304]{1,0:T(8,128)S(1)}, u32[]{:S(2)}, u32[]{:S(2)}) collective-permute-start(f32[48,2304]{1,0:T(8,128)S(1)} %get-tuple-element.16), channel_id=1, source_target_pairs={{0,32},{32,64},{64,96},{96,128},{128,160},{160,192},{192,224},{224... | collective-permute-start | bytes 1327112 | tf_op jit(solution)/shard_map/ppermute | solution.py:336
  19.5 9.8 %collective-permute-done = f32[48,2304]{1,0:T(8,128)S(1)} collective-permute-done((f32[48,2304]{1,0:T(8,128)S(1)}, f32[48,2304]{1,0:T(8,128)S(1)}, u32[]{:S(2)}, u32[]{:S(2)}) %collective-permute-start) | collective-permute-done | bytes 442400 | tf_op jit(solution)/shard_map/ppermute | solution.py:336
  29.3 0.1 maximum_bitcast_fusion
  29.4 0.6 copy.21
  30.0 32.1 %all_to_all.20 = f32[32,1,4608]{2,1,0:T(1,128)S(1)} all-to-all(f32[32,1,4608]{2,1,0:T(1,128)S(1)} %copy.21), channel_id=1, replica_groups=mesh['dom'=16,'orb'=32] {'orb'}, dimensions={0} | all-to-all | bytes 1179648 | tf_op jit(solution)/shard_map/all_to_all | solution.py:340
  62.1 0.3 reduce_sum.40
  62.5 0.7 slice_reduce_fusion
  63.2 0.2 broadcast_in_dim.42
  63.3 19.1 %all_to_all.21 = f32[32,1,2304]{2,1,0:T(1,128)S(1)} all-to-all(f32[32,1,2304]{2,1,0:T(1,128)S(1)} %broadcast_in_dim.42), channel_id=1, replica_groups=mesh['dom'=16,'orb'=32] {'orb'}, dimensions={0} | all-to-all | bytes 589824 | tf_op jit(solution)/shard_map/all_to_all | solution.py:345
  82.4 0.0 copy-start.1
  82.4 0.0 copy-start.3
  82.5 5.1 %collective-permute-start.1 = (f32[20,2304]{1,0:T(8,128)S(1)}, f32[20,2304]{1,0:T(8,128)S(1)}, u32[]{:S(2)}, u32[]{:S(2)}) collective-permute-start(f32[20,2304]{1,0:T(8,128)S(1)} %bitcast.29), channel_id=1, source_target_pairs={{32,0},{64,32},{96,64},{128,96},{160,128},{192,160},{224,192},{256... | collective-permute-start | bytes 552968 | tf_op jit(solution)/shard_map/ppermute | solution.py:347
  87.6 3.2 %collective-permute-done.1.high_ref = f32[20,2304]{1,0:T(8,128)S(1)} collective-permute-done((f32[20,2304]{1,0:T(8,128)S(1)}, f32[20,2304]{1,0:T(8,128)S(1)}, u32[]{:S(2)}, u32[]{:S(2)}) %collective-permute-start.1) | collective-permute-done | bytes 184352 | tf_op jit(solution)/shard_map/ppermute | solution.py:347
  90.9 0.0 copy-done.1
  90.9 0.0 copy-done.3
  90.9 10.6 %second.1 = (f32[32,2304]{1,0:T(8,128)S(1)}, f32[32,2304]{1,0:T(8,128)S(1)}, f32[24,2304]{1,0:T(8,128)S(1)}, f32[24,2304]{1,0:T(8,128)S(1)}, f32[1,128]{1,0:T(1,128)S(1)}) custom-call(f32[2]{0:T(128)S(1)} %fusion.3.factor_ref, s32[1]{0:T(128)} %bitcast.2.rank_ref, f32[2,48,2304]{2,1,0:T(8,128)S(1)} %get-tuple-element.14.psi_ref, f32[48,2304]{1,0:T(8,128)S(1)} %bitcast.26, ...), custom_call_target="tpu_custom_call" | custom-call | tf_op jit(solution)/shard_map/second/pallas_call | solution.py:349
  101.4 1.9 %collective-permute-start.2 = (f32[24,2304]{1,0:T(8,128)S(1)}, f32[24,2304]{1,0:T(8,128)S(1)}, u32[]{:S(2)}, u32[]{:S(2)}) collective-permute-start(f32[24,2304]{1,0:T(8,128)S(1)} %get-tuple-element.19), channel_id=1, source_target_pairs={{0,32},{32,64},{64,96},{96,128},{128,160},{160,192},{192,224},{224... | collective-permute-start | bytes 663560 | tf_op jit(solution)/shard_map/ppermute | solution.py:361
  103.4 5.9 %collective-permute-start.3 = (f32[24,2304]{1,0:T(8,128)S(1)}, f32[24,2304]{1,0:T(8,128)S(1)}, u32[]{:S(2)}, u32[]{:S(2)}) collective-permute-start(f32[24,2304]{1,0:T(8,128)S(1)} %get-tuple-element.20), channel_id=1, source_target_pairs={{32,0},{64,32},{96,64},{128,96},{160,128},{192,160},{224,192},{256... | collective-permute-start | bytes 663560 | tf_op jit(solution)/shard_map/ppermute | solution.py:362
  109.3 0.7 add_bitcast_fusion
  110.0 0.6 broadcast_in_dim.46
  110.6 3.5 %all-to-all-start.2 = ((f32[16,1,128]{2,1,0:T(1,128)}), f32[16,1,128]{2,1,0:T(1,128)S(1)}, u32[]{:S(2)}, u32[]{:S(2)}) async-start(f32[16,1,128]{2,1,0:T(1,128)} %broadcast_in_dim.46), calls=%async_computation.2 | async-start | bytes 16384 | tf_op jit(solution)/shard_map/all_to_all | solution.py:360
  114.1 5.9 %all-to-all-done.2 = f32[16,1,128]{2,1,0:T(1,128)S(1)} async-done(((f32[16,1,128]{2,1,0:T(1,128)}), f32[16,1,128]{2,1,0:T(1,128)S(1)}, u32[]{:S(2)}, u32[]{:S(2)}) %all-to-all-start.2) | async-done | bytes 8224 | tf_op jit(solution)/shard_map/all_to_all | solution.py:360
  120.0 0.0 collective-permute-done.2
  120.0 0.0 copy-start.6
  120.0 0.0 collective-permute-done.3
  120.1 0.6 copy-done.6
  120.7 0.0 slice-start
  120.7 0.9 slice-done
  121.7 0.6 copy.25
  122.3 27.9 %all_to_all.22 = f32[32,1,4736]{2,1,0:T(1,128)S(1)} all-to-all(f32[32,1,4736]{2,1,0:T(1,128)S(1)} %copy.25), channel_id=1, replica_groups=mesh['dom'=16,'orb'=32] {'orb'}, dimensions={0} | all-to-all | bytes 1212416 | tf_op jit(solution)/shard_map/all_to_all | solution.py:369
  150.2 0.3 reduce_sum.44
  150.6 0.5 slice.90
  151.7 0.7 fusion.2
  (19 shorter events, 0.4 us)
Async XLA Ops:
  0.7 0.7 copy-start.7
  1.3 0.8 copy-start.5
  1.4 0.7 copy-start.8
  2.1 1.0 copy-start
  3.1 1.0 copy-start.2
  4.1 1.2 copy-start.4
  17.5 11.7 %collective-permute-start = (f32[48,2304]{1,0:T(8,128)S(1)}, f32[48,2304]{1,0:T(8,128)S(1)}, u32[]{:S(2)}, u32[]{:S(2)}) collective-permute-start(f32[48,2304]{1,0:T(8,128)S(1)} %get-tuple-element.16), channel_id=1, source_target_pairs={{0,32},{32,64},{64,96},{96,128},{128,160},{160,192},{192,224},{224... | collective-permute-start | bytes 1327112 | tf_op jit(solution)/shard_map/ppermute | solution.py:336
  82.4 8.4 %copy-start.1 = (f32[1,48,2304]{2,1,0:T(8,128)S(1)}, f32[1,48,2304]{2,1,0:T(8,128)}, u32[]{:S(2)}) copy-start(f32[1,48,2304]{2,1,0:T(8,128)} %ext_ref.1) | copy-start | bytes 1327108
  82.4 8.4 %copy-start.3 = (f32[1,48,2304]{2,1,0:T(8,128)S(1)}, f32[1,48,2304]{2,1,0:T(8,128)}, u32[]{:S(2)}) copy-start(f32[1,48,2304]{2,1,0:T(8,128)} %core_ref.1) | copy-start | bytes 1327108
  82.5 8.4 %collective-permute-start.1 = (f32[20,2304]{1,0:T(8,128)S(1)}, f32[20,2304]{1,0:T(8,128)S(1)}, u32[]{:S(2)}, u32[]{:S(2)}) collective-permute-start(f32[20,2304]{1,0:T(8,128)S(1)} %bitcast.29), channel_id=1, source_target_pairs={{32,0},{64,32},{96,64},{128,96},{160,128},{192,160},{224,192},{256... | collective-permute-start | bytes 552968 | tf_op jit(solution)/shard_map/ppermute | solution.py:347
  101.4 18.5 %collective-permute-start.2 = (f32[24,2304]{1,0:T(8,128)S(1)}, f32[24,2304]{1,0:T(8,128)S(1)}, u32[]{:S(2)}, u32[]{:S(2)}) collective-permute-start(f32[24,2304]{1,0:T(8,128)S(1)} %get-tuple-element.19), channel_id=1, source_target_pairs={{0,32},{32,64},{64,96},{96,128},{128,160},{160,192},{192,224},{224... | collective-permute-start | bytes 663560 | tf_op jit(solution)/shard_map/ppermute | solution.py:361
  103.4 16.6 %collective-permute-start.3 = (f32[24,2304]{1,0:T(8,128)S(1)}, f32[24,2304]{1,0:T(8,128)S(1)}, u32[]{:S(2)}, u32[]{:S(2)}) collective-permute-start(f32[24,2304]{1,0:T(8,128)S(1)} %get-tuple-element.20), channel_id=1, source_target_pairs={{32,0},{64,32},{96,64},{128,96},{160,128},{192,160},{224,192},{256... | collective-permute-start | bytes 663560 | tf_op jit(solution)/shard_map/ppermute | solution.py:362
  110.6 9.4 %all-to-all-start.2 = ((f32[16,1,128]{2,1,0:T(1,128)}), f32[16,1,128]{2,1,0:T(1,128)S(1)}, u32[]{:S(2)}, u32[]{:S(2)}) async-start(f32[16,1,128]{2,1,0:T(1,128)} %broadcast_in_dim.46), calls=%async_computation.2 | async-start | bytes 16384 | tf_op jit(solution)/shard_map/all_to_all | solution.py:360
  120.0 0.7 copy-start.6
  120.7 0.9 slice-start

commit v2 on v1

--- a/solution.py
+++ b/solution.py
@@ -2,6 +2,8 @@
 
 import jax
 import jax.numpy as jnp
+import ml_dtypes
+import numpy as np
 from jax import lax
 from jax.experimental import pallas as pl
 from jax.experimental.pallas import tpu as pltpu
@@ -17,7 +19,6 @@
 LANES = 128
 COLS = CELLS // LANES
 PAD = 8
-EXT = 64
 SHIFT = 12
 UP = 20
 BLOCK = 384
@@ -34,23 +35,19 @@
 SOURCE = SPREAD * FOUR_PI
 
 
-def build_neighbours(matrix_ref):
-    rows = lax.broadcasted_iota(jnp.int32, (DEPTH, BLOCK), 0)
-    cols = lax.broadcasted_iota(jnp.int32, (DEPTH, BLOCK), 1)
+def neighbour_matrix():
+    rows = np.arange(DEPTH)[:, None]
+    cols = np.arange(BLOCK)[None, :]
     edge = rows - BLOCK
-    inside = rows < BLOCK
     after = edge < SIDE
     before = edge >= LANES - SIDE
-    row_y = jnp.where(inside, rows // SIDE, jnp.where(after, SIDE // 6, jnp.where(before, -1, -9)))
-    row_x = jnp.where(inside, rows % SIDE, jnp.where(after, edge, edge - (LANES - SIDE)))
-    col_y = cols // SIDE
-    col_x = cols % SIDE
-    gap_x = jnp.abs(row_x - col_x)
-    along = (row_y == col_y) & ((gap_x == 1) | (gap_x == SIDE - 1))
-    across = (row_x == col_x) & (jnp.abs(row_y - col_y) == 1)
-    ones = jnp.where(along | across, 1.0, 0.0).astype(jnp.bfloat16)
-    matrix_ref[0:DEPTH, :] = ones
-    matrix_ref[DEPTH : 2 * DEPTH, :] = ones
+    row_y = np.where(rows < BLOCK, rows // SIDE, np.where(after, BLOCK // SIDE, np.where(before, -1, -9)))
+    row_x = np.where(rows < BLOCK, rows % SIDE, np.where(after, edge, edge - (LANES - SIDE)))
+    gap_x = np.abs(row_x - cols % SIDE)
+    along = (row_y == cols // SIDE) & ((gap_x == 1) | (gap_x == SIDE - 1))
+    across = (gap_x == 0) & (np.abs(row_y - cols // SIDE) == 1)
+    ones = (along | across).astype(ml_dtypes.bfloat16)
+    return np.concatenate([ones, ones], axis=0)
 
 
 def tile_of(ref, start):
@@ -200,101 +197,138 @@
     return [weight * d for d in total]
 
 
-def relax(plane_ref, row, g_ref, h_ref, d_ref, split_ref, sum_ref, matrix_ref):
-    clear_pads((g_ref, h_ref), EXT)
-    g_ref[PAD : PAD + EXT, :] = jnp.zeros((EXT, CELLS), jnp.float32)
-    g_ref[pl.ds(PAD + row, 1), :] = plane_ref[...]
-
+def place_plane(g_ref, plane, row, wanted):
+    @pl.when(wanted)
+    def _():
+        g_ref[pl.ds(PAD + row, 1), :] = plane[...]
+
+
+def relax(g_ref, h_ref, d_ref, split_ref, sum_ref, matrix_ref):
     def rule(r, here, total):
         push = tile_of(d_ref, r)
         return [KEEP * here[i] + SPREAD * total[i] + SOURCE * push[i] for i in range(COLS)]
 
     def one(source, target, last=False):
-        multiply(split_ref, matrix_ref, sum_ref, BLOCKS * EXT)
-        update(source, target, None if last else split_ref, sum_ref, EXT, rule)
-
-    split_all(g_ref, split_ref, EXT)
+        multiply(split_ref, matrix_ref, sum_ref, BLOCKS * BOX)
+        update(source, target, None if last else split_ref, sum_ref, BOX, rule)
+
+    split_all(g_ref, split_ref, BOX)
     for k in range(SWEEPS // 2):
         one(g_ref, h_ref)
         one(h_ref, g_ref, last=k == SWEEPS // 2 - 1)
 
 
-def first_kernel(
-    share, factor_ref, rank_ref, orbitals_ref, ext_ref, core_ref, weight_ref, guess_ref,
-    psi_out, frame_out, smooth_out, up_out,
-    a0, a1, b0, b1, x0, x1, s0, s1, w_ref, g_ref, h_ref, d_ref, matrix_ref, v_ref, c_ref, sem,
+def first_filter(
+    share, factor_ref, orbitals_ref, ext_ref, core_ref, matrix_hbm, weight_ref, guess_ref,
+    psi_out, density_out, up_out,
+    a0, a1, b0, b1, x0, x1, s0, s1, w_ref, matrix_ref, v_ref, c_ref, sem,
 ):
     copies = [
         pltpu.make_async_copy(ext_ref.at[0], v_ref, sem.at[0]),
         pltpu.make_async_copy(orbitals_ref.at[0, 0], a0.at[PAD : PAD + BOX], sem.at[1]),
         pltpu.make_async_copy(orbitals_ref.at[0, 1], a1.at[PAD : PAD + BOX], sem.at[2]),
-        pltpu.make_async_copy(core_ref.at[0], c_ref, sem.at[3]),
+        pltpu.make_async_copy(matrix_hbm, matrix_ref, sem.at[3]),
+        pltpu.make_async_copy(core_ref.at[0], c_ref, sem.at[4]),
     ]
     for copy in copies:
         copy.start()
-    build_neighbours(matrix_ref)
     clear_pads((a0, a1, b0, b1), BOX)
     copies[0].wait()
     single = scaled_potential(lambda r: tile_of(v_ref, r), w_ref)
-    copies[1].wait()
-    copies[2].wait()
+    for copy in copies[1:4]:
+        copy.wait()
     run_filter((a0, a1), (b0, b1), (x0, x1), (s0, s1), matrix_ref, w_ref, single)
     scale = norms((a0, a1))
-    copies[3].wait()
-    zero = jnp.zeros((8, CELLS), jnp.float32)
-    d_ref[0:8, :] = zero
-    d_ref[56:64, :] = zero
-    for t in range(BOX // 8):
-        put_tile(d_ref, 8 + 8 * t, density_tile((a0, a1), scale, factor_ref, c_ref, weight_ref, t, share, psi_out))
-    relax(guess_ref, 16 + rank_ref[0], g_ref, h_ref, d_ref, x0, s0, matrix_ref)
+    copies[4].wait()
+    for t in range(BOX // 8):
+        put_tile(density_out, 8 * t, density_tile((a0, a1), scale, factor_ref, c_ref, weight_ref, t, share, psi_out))
+    up_out[0:1, :] = guess_ref[...]
+    up_out[1:24, :] = density_out[25:48, :]
+
+
+def first_relax(rank_ref, density_ref, behind_ref, guess_ref, matrix_ref, out_ref, g_ref, h_ref, d_ref, x0, s0):
+    clear_pads((g_ref, h_ref), BOX)
+    rank = rank_ref[0]
+    row = lax.broadcasted_iota(jnp.int32, (8, LANES), 0)
+    for t in range(BOX // 8):
+        total = None
+        if t >= 1:
+            total = tile_of(density_ref, 8 * (t - 1))
+        if t < 3:
+            behind = tile_of(behind_ref, 8 * t)
+            if t == 0:
+                total = [jnp.where(row > 0, b, 0.0) for b in behind]
+            else:
+                total = [total[i] + behind[i] for i in range(COLS)]
+        put_tile(d_ref, 8 * t, total)
+    g_ref[PAD : PAD + BOX, :] = jnp.zeros((BOX, CELLS), jnp.float32)
+    g_ref[pl.ds(PAD + 16 + rank, 1), :] = guess_ref[...]
+    place_plane(g_ref, behind_ref.at[0:1, :], rank - 16, rank >= 16)
+    relax(g_ref, h_ref, d_ref, x0, s0, matrix_ref)
     low = 16 - SHIFT
-    frame_out[...] = d_ref[low : low + CORE, :]
-    smooth_out[...] = g_ref[PAD + low : PAD + low + CORE, :]
-    up_out[0:UP, :] = d_ref[low + CORE : low + CORE + UP, :]
-    up_out[UP : 48, :] = g_ref[PAD + low + CORE : PAD + EXT, :]
-
-
-def second_kernel(
-    share, factor_ref, rank_ref, psi_ref, ext_ref, core_ref, weight_ref, plane_ref, low_ref, high_ref,
-    core_out, smooth_out, up_out, down_out, charge_out,
-    a0, a1, b0, b1, x0, x1, s0, s1, w_ref, g_ref, h_ref, d_ref, matrix_ref,
+    for p in range(CORE):
+        out_ref[p, :, 0:CELLS] = d_ref[low + p : low + p + 1, :]
+        out_ref[p, :, CELLS : 2 * CELLS] = g_ref[PAD + low + p : PAD + low + p + 1, :]
+
+
+def second_filter(
+    share, factor_ref, psi_ref, ext_ref, core_ref, weight_ref, low_ref, high_ref, owned_ref, matrix_ref,
+    density_out, up_out, down_out, charge_out,
+    a0, a1, b0, b1, x0, x1, s0, s1, w_ref, v_ref,
 ):
-    build_neighbours(matrix_ref)
     clear_pads((a0, a1, b0, b1), BOX)
     a0[PAD : PAD + BOX, :] = psi_ref[0]
     a1[PAD : PAD + BOX, :] = psi_ref[1]
     first = SHIFT - BUF
-    h_ref[0 : CORE - first, :] = low_ref[first:CORE, :]
-    h_ref[CORE - first : BOX, :] = high_ref[...]
+    v_ref[0 : CORE - first, :] = low_ref[first:CORE, :]
+    v_ref[CORE - first : BOX, :] = high_ref[0:UP, :]
     for t in range(BOX // 8):
         ionic = tile_of(ext_ref, 8 * t)
-        own = tile_of(h_ref, 8 * t)
-        put_tile(h_ref, 8 * t, [ionic[i] + own[i] for i in range(COLS)])
-    single = scaled_potential(lambda r: tile_of(h_ref, r), w_ref)
+        own = tile_of(v_ref, 8 * t)
+        put_tile(v_ref, 8 * t, [ionic[i] + own[i] for i in range(COLS)])
+    single = scaled_potential(lambda r: tile_of(v_ref, r), w_ref)
     run_filter((a0, a1), (b0, b1), (x0, x1), (s0, s1), matrix_ref, w_ref, single)
     scale = norms((a0, a1))
-    zero = jnp.zeros((8, CELLS), jnp.float32)
-    d_ref[0:8, :] = zero
-    d_ref[56:64, :] = zero
     charge = [jnp.zeros((8, LANES), jnp.float32) for _ in range(3)]
     for t in range(BOX // 8):
         tile = density_tile((a0, a1), scale, factor_ref, core_ref, weight_ref, t, share, None)
-        put_tile(d_ref, 8 + 8 * t, tile)
+        put_tile(density_out, 8 * t, tile)
         for i, d in enumerate(tile):
             charge[i % 3] = charge[i % 3] + d
-    charge_out[...] = jnp.broadcast_to(jnp.sum(charge[0] + charge[1] + charge[2], keepdims=True), charge_out.shape)
-    relax(plane_ref, 16 - SHIFT + rank_ref[0], g_ref, h_ref, d_ref, x0, s0, matrix_ref)
-    core_out[...] = d_ref[16:48, :]
-    down_out[0:8, :] = d_ref[8:16, :]
-    up_out[0:8, :] = d_ref[48:56, :]
-    down_out[8:24, :] = g_ref[PAD : PAD + 16, :]
-    smooth_out[...] = g_ref[PAD + 16 : PAD + 48, :]
-    up_out[8:24, :] = g_ref[PAD + 48 : PAD + 64, :]
+    charge = jnp.sum(charge[0] + charge[1] + charge[2], keepdims=True) + jnp.sum(owned_ref[...], keepdims=True)
+    charge_out[...] = jnp.broadcast_to(charge[None], charge_out.shape)
+    down_out[...] = density_out[0:16, :]
+    up_out[...] = density_out[32:48, :]
+
+
+def second_relax(
+    rank_ref, density_ref, below_ref, above_ref, plane_ref, high_ref, charge_ref, matrix_ref, out_ref,
+    g_ref, h_ref, d_ref, x0, s0,
+):
+    clear_pads((g_ref, h_ref), BOX)
+    rank = rank_ref[0]
+    for t in range(BOX // 8):
+        total = tile_of(density_ref, 8 * t)
+        if t < 2:
+            below = tile_of(below_ref, 8 * t)
+            total = [total[i] + below[i] for i in range(COLS)]
+        if t >= 4:
+            above = tile_of(above_ref, 8 * (t - 4))
+            total = [total[i] + above[i] for i in range(COLS)]
+        put_tile(d_ref, 8 * t, total)
+    g_ref[PAD : PAD + BOX, :] = jnp.zeros((BOX, CELLS), jnp.float32)
+    place_plane(g_ref, plane_ref, rank - (SHIFT - BUF), rank >= SHIFT - BUF)
+    place_plane(g_ref, high_ref.at[UP : UP + 1, :], rank + CORE - SHIFT + BUF, rank < BOX - (CORE - SHIFT + BUF))
+    relax(g_ref, h_ref, d_ref, x0, s0, matrix_ref)
+    for p in range(CORE):
+        out_ref[p, :, 0:CELLS] = d_ref[BUF + p : BUF + p + 1, :]
+        out_ref[p, :, CELLS : 2 * CELLS] = g_ref[PAD + BUF + p : PAD + BUF + p + 1, :]
+        out_ref[p, :, 2 * CELLS : 2 * CELLS + LANES] = charge_ref[...]
 
 
 VMEM = pl.BlockSpec(memory_space=pltpu.VMEM)
 SMEM = pl.BlockSpec(memory_space=pltpu.SMEM)
-ANY = pl.BlockSpec(memory_space=pl.ANY)
+HBM = pl.BlockSpec(memory_space=pltpu.HBM)
 LIMIT = pltpu.CompilerParams(vmem_limit_bytes=48 * 2**20)
 
 
@@ -314,60 +348,66 @@
     share = 1.0 / orb_count
     up = [(i, (i + 1) % dom_count) for i in range(dom_count)]
     down = [(j, i) for i, j in up]
+    matrix = jnp.asarray(neighbour_matrix())
     padded = pltpu.VMEM((BOX + 2 * PAD, CELLS), jnp.float32)
-    wide = pltpu.VMEM((EXT + 2 * PAD, CELLS), jnp.float32)
-    split = pltpu.VMEM((BLOCKS * EXT, 2 * DEPTH), jnp.bfloat16)
-    sums = pltpu.VMEM((BLOCKS * EXT, BLOCK), jnp.float32)
+    split = pltpu.VMEM((BLOCKS * BOX, 2 * DEPTH), jnp.bfloat16)
+    sums = pltpu.VMEM((BLOCKS * BOX, BLOCK), jnp.float32)
     box = pltpu.VMEM((BOX, CELLS), jnp.float32)
-    scratch = [padded] * 4 + [split] * 2 + [sums] * 2 + [
-        box, wide, wide, pltpu.VMEM((EXT, CELLS), jnp.float32), pltpu.VMEM((2 * DEPTH, BLOCK), jnp.bfloat16)
-    ]
-
-    psi, frame, smooth, upper = pl.pallas_call(
-        functools.partial(first_kernel, share),
-        in_specs=[SMEM] * 2 + [ANY] * 3 + [VMEM] * 2,
-        out_specs=[VMEM] * 4,
-        out_shape=[f32(per_device, BOX, CELLS), f32(CORE, CELLS), f32(CORE, CELLS), f32(48, CELLS)],
-        scratch_shapes=scratch + [box, box, pltpu.SemaphoreType.DMA((4,))],
+    whole = pltpu.VMEM((2 * DEPTH, BLOCK), jnp.bfloat16)
+    filter_scratch = [padded] * 4 + [split] * 2 + [sums] * 2 + [box]
+    relax_scratch = [padded, padded, box, split, sums]
+
+    psi, density, upper = pl.pallas_call(
+        functools.partial(first_filter, share),
+        in_specs=[SMEM] + [HBM] * 4 + [VMEM] * 2,
+        out_specs=[VMEM] * 3,
+        out_shape=[f32(per_device, BOX, CELLS), f32(BOX, CELLS), f32(24, CELLS)],
+        scratch_shapes=filter_scratch + [whole, box, box, pltpu.SemaphoreType.DMA((5,))],
         compiler_params=LIMIT,
-        name="first",
-    )(factors, place, orbitals, external_potential, core_density, weight, hartree_guess)
+        name="first_filter",
+    )(factors, orbitals, external_potential, core_density, matrix, weight, hartree_guess)
 
     behind = lax.ppermute(upper, "dom", up)
-    frame = jnp.concatenate([frame[:UP] + behind[:UP], frame[UP:]], axis=0)
-    smooth = jnp.concatenate([smooth[:28] + behind[UP:], smooth[28:]], axis=0)
-    sent = jnp.concatenate([frame[:, None], smooth[:, None]], axis=2)
-    arrived = lax.all_to_all(sent, "orb", 0, 0, tiled=True)
-    total = arrived.sum(axis=0)
+    sent = pl.pallas_call(
+        first_relax,
+        in_specs=[SMEM] + [VMEM] * 4,
+        out_specs=VMEM,
+        out_shape=f32(orb_count, 1, 2 * CELLS),
+        scratch_shapes=relax_scratch,
+        compiler_params=LIMIT,
+        name="first_relax",
+    )(place, density, behind, hartree_guess, matrix)
+    total = lax.all_to_all(sent, "orb", 0, 0, tiled=True).sum(axis=0)
     owned_density = total[:, :CELLS]
     owned_hartree = total[:, CELLS:]
     plane = owned_hartree - EXCHANGE_FACTOR * jnp.cbrt(owned_density)
     low = lax.all_to_all(jnp.broadcast_to(plane[None], (orb_count, 1, CELLS)), "orb", 0, 0, tiled=True)
     low = low.reshape(CORE, CELLS)
-    high = lax.ppermute(low[:UP], "dom", down)
-
-    core, smooth, upper, lower, charge = pl.pallas_call(
-        functools.partial(second_kernel, share),
-        in_specs=[SMEM] * 2 + [VMEM] * 7,
-        out_specs=[VMEM] * 5,
-        out_shape=[f32(CORE, CELLS), f32(CORE, CELLS), f32(24, CELLS), f32(24, CELLS), f32(1, LANES)],
-        scratch_shapes=scratch,
+    high = lax.ppermute(jnp.concatenate([low[:UP], owned_hartree], axis=0), "dom", down)
+
+    density, upper, lower, charge = pl.pallas_call(
+        functools.partial(second_filter, share),
+        in_specs=[SMEM] + [VMEM] * 8,
+        out_specs=[VMEM] * 4,
+        out_shape=[f32(BOX, CELLS), f32(16, CELLS), f32(16, CELLS), f32(dom_count, 1, LANES)],
+        scratch_shapes=filter_scratch + [box],
         compiler_params=LIMIT,
-        name="second",
-    )(factors, place, psi, external_potential[0], core_density[0], weight, owned_hartree, low, high)
-
-    charge = charge + jnp.sum(owned_density)
-    charge = lax.all_to_all(jnp.broadcast_to(charge[None], (dom_count, 1, LANES)), "dom", 0, 0, tiled=True)
+        name="second_filter",
+    )(factors, psi, external_potential[0], core_density[0], weight, low, high, owned_density, matrix)
+
+    charge = lax.all_to_all(charge, "dom", 0, 0, tiled=True).sum(axis=0)
     from_below = lax.ppermute(upper, "dom", up)
     from_above = lax.ppermute(lower, "dom", down)
-    charge = charge.sum(axis=0)
-    core = jnp.concatenate([core[:8] + from_below[:8], core[8:24], core[24:] + from_above[:8]], axis=0)
-    smooth = smooth + jnp.concatenate([from_below[8:], from_above[8:]], axis=0)
-    sent = jnp.concatenate(
-        [core[:, None], smooth[:, None], jnp.broadcast_to(charge[None], (orb_count, 1, LANES))], axis=2
-    )
-    arrived = lax.all_to_all(sent, "orb", 0, 0, tiled=True)
-    total = arrived.sum(axis=0)
+    sent = pl.pallas_call(
+        second_relax,
+        in_specs=[SMEM] + [VMEM] * 7,
+        out_specs=VMEM,
+        out_shape=f32(orb_count, 1, 2 * CELLS + LANES),
+        scratch_shapes=relax_scratch,
+        compiler_params=LIMIT,
+        name="second_relax",
+    )(place, density, from_below, from_above, owned_hartree, high, charge, matrix)
+    total = lax.all_to_all(sent, "orb", 0, 0, tiled=True).sum(axis=0)
     density = total[:, :CELLS]
     average = total[:, 2 * CELLS : 2 * CELLS + 1] / (dom_count * CORE * CELLS)
     return total[:, CELLS : 2 * CELLS] - (SWEEPS * SOURCE) * average - EXCHANGE_FACTOR * jnp.cbrt(density)

time: 153 us -> 145 us (0.948)
  blocking collectives: 79 us -> 87.7 us
  waiting for transfers between devices: 18.9 us -> 10.8 us
  starting transfers between devices: 18.4 us -> 14.7 us
  local copies, waits for them, and re-layouts: 8.75 us -> 6.49 us
    all_to_all x2 -> x3, blocking collectives: 60 us -> 68.6 us  [the longest x2 60 us: body(): total = lax.all_to_all(sent, 'orb', 0, 0, tiled=True).sum(axis=0)]
    all_to_all x1 -> x0, waiting for transfers between devices: 5.89 us -> none  [body(): lax.all_to_all(jnp.broadcast_to(charge[None], (dom_count, 1, LANES)), 'do...]
    all_to_all x1 -> x0, starting transfers between devices: 3.47 us -> none  [body(): lax.all_to_all(jnp.broadcast_to(charge[None], (dom_count, 1, LANES)), 'do...]
    ppermute x1, waiting for transfers between devices: 9.76 us -> 7.43 us  [body(): behind = lax.ppermute(upper, 'dom', up)]
    pallas_call x2 -> x4, Pallas kernels: 22.8 us -> 22.1 us  [the longest x1 9.52 us: body(): pl.pallas_call(functools.partial(first_filter, share), in_specs=[SMEM] +...]
    unnamed x20 -> x22, local copies, waits for them, and re-layouts: 5.16 us -> 5.68 us
  transfers between devices with their start and end apart: 5 -> 4, of which waited for: 3 -> 2; matrix products, arithmetic and copies ran while one was open for 1% -> 0% of each run, Pallas kernels for 0% -> 0%
where the time goes in v2:
time: 145 us
  blocking collectives  87.7 us (60%)
  Pallas kernels  22.1 us (15%)
  starting transfers between devices  14.7 us (10%)
  waiting for transfers between devices  10.8 us (7%)
  local copies, waits for them, and re-layouts  6.49 us (4%)
  other arithmetic  1.52 us (1%)
  between operations  1.48 us (1%)
    all_to_all x2, blocking collectives, body(): total = lax.all_to_all(sent, 'orb', 0, 0, tiled=True).sum(axis=0)  60 us
    all_to_all x1, blocking collectives, body(): lax.all_to_all(jnp.broadcast_to(plane[None], (orb_count, 1, CELLS)), 'orb...  19 us
    pallas_call x1, Pallas kernels, body(): pl.pallas_call(functools.partial(first_filter, share), in_specs=[SMEM] +...  9.52 us
    all_to_all x1, blocking collectives, body(): charge = lax.all_to_all(charge, 'dom', 0, 0, tiled=True).sum(axis=0)  8.6 us
    pallas_call x1, Pallas kernels, body(): pl.pallas_call(functools.partial(second_filter, share), in_specs=[SMEM] +...  8.22 us
    ppermute x1, waiting for transfers between devices, body(): behind = lax.ppermute(upper, 'dom', up)  7.43 us
    ppermute x1, starting transfers between devices, body(): from_above = lax.ppermute(lower, 'dom', down)  5.92 us
    unnamed x22, local copies, waits for them, and re-layouts  5.68 us
  transfers between devices with their start and end apart: 4, of which 2 were waited for; matrix products, arithmetic and copies ran while one was open for 0% of the time, Pallas kernels for 0%

profile of v2, /device:TPU:64, one launch (start us, length us, event | category | flops | bytes accessed | tf_op | source)
XLA Modules:
  0.0 144.8 jit_solution(6211359380478837620)
XLA Ops:
  0.7 0.0 copy-start.8
  0.7 0.6 copy-done.8
  1.3 0.0 copy-start.7
  1.3 0.1 copy.11.weight_ref
  1.4 0.0 copy-start.9
  1.4 0.7 copy-done.9
  2.1 0.0 copy-done.7
  2.1 0.0 copy-start
  2.1 1.1 copy-done
  3.2 0.0 copy-start.2
  3.2 1.0 copy-done.2
  4.2 0.0 copy-start.4
  4.2 1.0 copy-done.4
  5.2 0.0 copy-start.6
  5.2 1.2 copy-done.6
  6.4 0.0 copy-start.1
  6.4 9.5 %first_filter.1 = (f32[2,48,2304]{2,1,0:T(8,128)S(1)}, f32[48,2304]{1,0:T(8,128)S(1)}, f32[24,2304]{1,0:T(8,128)S(1)}) custom-call(f32[2]{0:T(128)S(1)} %fusion.2.factor_ref, f32[1,2,48,2304]{3,2,1,0:T(8,128)S(1)} %copy-done.6, f32[1,48,2304]{2,1,0:T(8,128)S(1)} %copy-done.2, f32[1,48,2304]{2,1,0:T(8,128)S(1)} %copy-done.4, bf16[1024,384]{1,0:T(8,128)(2,1)S(1)} %copy-done, ...), custom_call_target="tpu_custom_call" | custom-call | tf_op jit(solution)/shard_map/first_filter/pallas_call | solution.py:360
  15.9 1.9 %collective-permute-start = (f32[24,2304]{1,0:T(8,128)S(1)}, f32[24,2304]{1,0:T(8,128)S(1)}, u32[]{:S(2)}, u32[]{:S(2)}) collective-permute-start(f32[24,2304]{1,0:T(8,128)S(1)} %get-tuple-element.14), channel_id=1, source_target_pairs={{0,32},{32,64},{64,96},{96,128},{128,160},{160,192},{192,224},{224... | collective-permute-start | bytes 663560 | tf_op jit(solution)/shard_map/ppermute | solution.py:370
  17.9 7.4 %collective-permute-done.behind_ref = f32[24,2304]{1,0:T(8,128)S(1)} collective-permute-done((f32[24,2304]{1,0:T(8,128)S(1)}, f32[24,2304]{1,0:T(8,128)S(1)}, u32[]{:S(2)}, u32[]{:S(2)}) %collective-permute-start) | collective-permute-done | bytes 221216 | tf_op jit(solution)/shard_map/ppermute | solution.py:370
  25.3 0.0 copy-done.1
  25.3 2.2 %first_relax.1 = f32[32,1,4608]{2,1,0:T(1,128)S(1)} custom-call(s32[1]{0:T(128)} %bitcast.rank_ref, f32[48,2304]{1,0:T(8,128)S(1)} %get-tuple-element.13.density_ref, f32[24,2304]{1,0:T(8,128)S(1)} %collective-permute-done.behind_ref, f32[1,2304]{1,0:T(1,128)S(1)} %copy-done.7, bf16[1024,384]{1,0:T(8,128)(2,1)S(1)} %copy-done.1), custom_call_target="tpu_custom_call" | custom-call | tf_op jit(solution)/shard_map/first_relax/pallas_call | solution.py:371
  27.5 32.1 %all_to_all.20 = f32[32,1,4608]{2,1,0:T(1,128)S(1)} all-to-all(f32[32,1,4608]{2,1,0:T(1,128)S(1)} %first_relax.1), channel_id=1, replica_groups=mesh['dom'=16,'orb'=32] {'orb'}, dimensions={0} | all-to-all | bytes 1179648 | tf_op jit(solution)/shard_map/all_to_all | solution.py:380
  59.6 0.3 reduce_sum.33
  60.0 0.1 fusion.3
  60.1 0.2 broadcast_in_dim.14
  60.2 19.0 %all_to_all.21 = f32[32,1,2304]{2,1,0:T(1,128)S(1)} all-to-all(f32[32,1,2304]{2,1,0:T(1,128)S(1)} %broadcast_in_dim.14), channel_id=1, replica_groups=mesh['dom'=16,'orb'=32] {'orb'}, dimensions={0} | all-to-all | bytes 589824 | tf_op jit(solution)/shard_map/all_to_all | solution.py:384
  79.3 0.0 copy-start.3
  79.3 0.0 copy-start.5
  79.4 5.0 %collective-permute-start.1 = (f32[21,2304]{1,0:T(8,128)S(1)}, f32[21,2304]{1,0:T(8,128)S(1)}, u32[]{:S(2)}, u32[]{:S(2)}) collective-permute-start(f32[21,2304]{1,0:T(8,128)S(1)} %pad_maximum_fusion), channel_id=1, source_target_pairs={{32,0},{64,32},{96,64},{128,96},{160,128},{192,160},{224,192},{256... | collective-permute-start | bytes 580616 | tf_op jit(solution)/shard_map/ppermute | solution.py:386
  84.4 3.4 %collective-permute-done.1.high_ref = f32[21,2304]{1,0:T(8,128)S(1)} collective-permute-done((f32[21,2304]{1,0:T(8,128)S(1)}, f32[21,2304]{1,0:T(8,128)S(1)}, u32[]{:S(2)}, u32[]{:S(2)}) %collective-permute-start.1) | collective-permute-done | bytes 193568 | tf_op jit(solution)/shard_map/ppermute | solution.py:386
  87.8 0.0 copy-done.3
  87.8 0.0 copy-done.5
  87.8 8.2 %second_filter.1 = (f32[48,2304]{1,0:T(8,128)S(1)}, f32[16,2304]{1,0:T(8,128)S(1)}, f32[16,2304]{1,0:T(8,128)S(1)}, f32[16,1,128]{2,1,0:T(1,128)S(1)}) custom-call(f32[2]{0:T(128)S(1)} %fusion.2.factor_ref, f32[2,48,2304]{2,1,0:T(8,128)S(1)} %get-tuple-element.12.psi_ref, f32[48,2304]{1,0:T(8,128)S(1)} %bitcast.16, f32[48,2304]{1,0:T(8,128)S(1)} %bitcast.17, ...), custom_call_target="tpu_custom_call" | custom-call | tf_op jit(solution)/shard_map/second_filter/pallas_call | solution.py:388
  96.0 1.9 %collective-permute-start.2 = (f32[16,2304]{1,0:T(8,128)S(1)}, f32[16,2304]{1,0:T(8,128)S(1)}, u32[]{:S(2)}, u32[]{:S(2)}) collective-permute-start(f32[16,2304]{1,0:T(8,128)S(1)} %get-tuple-element.16), channel_id=1, source_target_pairs={{0,32},{32,64},{64,96},{96,128},{128,160},{160,192},{192,224},{224... | collective-permute-start | bytes 442376 | tf_op jit(solution)/shard_map/ppermute | solution.py:399
  97.9 5.9 %collective-permute-start.3 = (f32[16,2304]{1,0:T(8,128)S(1)}, f32[16,2304]{1,0:T(8,128)S(1)}, u32[]{:S(2)}, u32[]{:S(2)}) collective-permute-start(f32[16,2304]{1,0:T(8,128)S(1)} %get-tuple-element.17), channel_id=1, source_target_pairs={{32,0},{64,32},{96,64},{128,96},{160,128},{192,160},{224,192},{256... | collective-permute-start | bytes 442376 | tf_op jit(solution)/shard_map/ppermute | solution.py:400
  103.9 8.6 %all_to_all.22 = f32[16,1,128]{2,1,0:T(1,128)S(1)} all-to-all(f32[16,1,128]{2,1,0:T(1,128)S(1)} %get-tuple-element.18), channel_id=1, replica_groups=mesh['dom'=16,'orb'=32] {'dom'}, dimensions={0} | all-to-all | bytes 16384 | tf_op jit(solution)/shard_map/all_to_all | solution.py:398
  112.5 0.0 collective-permute-done.2.below_ref
  112.5 0.0 collective-permute-done.3.above_ref
  112.5 2.2 %second_relax.1 = f32[32,1,4736]{2,1,0:T(1,128)S(1)} custom-call(s32[1]{0:T(128)} %bitcast.rank_ref, f32[48,2304]{1,0:T(8,128)S(1)} %get-tuple-element.15.density_ref, f32[16,2304]{1,0:T(8,128)S(1)} %collective-permute-done.2.below_ref, f32[16,2304]{1,0:T(8,128)S(1)} %collective-permute-done.3.above_ref, f32[1,2304]{1,0:T(1,128)S(1)} %get-tuple-element.21.plane_ref, ...), custom_call_target="tpu_custom_call" | custom-call | tf_op jit(solution)/shard_map/second_relax/pallas_call | solution.py:401
  114.7 27.9 %all_to_all.23 = f32[32,1,4736]{2,1,0:T(1,128)S(1)} all-to-all(f32[32,1,4736]{2,1,0:T(1,128)S(1)} %second_relax.1), channel_id=1, replica_groups=mesh['dom'=16,'orb'=32] {'orb'}, dimensions={0} | all-to-all | bytes 1212416 | tf_op jit(solution)/shard_map/all_to_all | solution.py:410
  142.6 0.3 reduce_sum.37
  143.0 0.5 slice.32
  144.2 0.7 fusion.1
  (8 shorter events, 0.2 us)
Async XLA Ops:
  0.7 0.7 copy-start.8
  1.3 0.8 copy-start.7
  1.4 0.7 copy-start.9
  2.1 1.1 copy-start
  3.2 1.0 copy-start.2
  4.2 1.0 copy-start.4
  5.2 1.2 copy-start.6
  6.4 18.9 %copy-start.1 = (bf16[1024,384]{1,0:T(8,128)(2,1)S(1)}, bf16[1024,384]{1,0:T(8,128)(2,1)}, u32[]{:S(2)}) copy-start(bf16[1024,384]{1,0:T(8,128)(2,1)} %constant.20.clone.matrix_hbm.matrix_ref) | copy-start | bytes 2359300
  15.9 9.4 %collective-permute-start = (f32[24,2304]{1,0:T(8,128)S(1)}, f32[24,2304]{1,0:T(8,128)S(1)}, u32[]{:S(2)}, u32[]{:S(2)}) collective-permute-start(f32[24,2304]{1,0:T(8,128)S(1)} %get-tuple-element.14), channel_id=1, source_target_pairs={{0,32},{32,64},{64,96},{96,128},{128,160},{160,192},{192,224},{224... | collective-permute-start | bytes 663560 | tf_op jit(solution)/shard_map/ppermute | solution.py:370
  79.3 8.4 %copy-start.3 = (f32[1,48,2304]{2,1,0:T(8,128)S(1)}, f32[1,48,2304]{2,1,0:T(8,128)}, u32[]{:S(2)}) copy-start(f32[1,48,2304]{2,1,0:T(8,128)} %ext_ref.1) | copy-start | bytes 1327108
  79.3 8.4 %copy-start.5 = (f32[1,48,2304]{2,1,0:T(8,128)S(1)}, f32[1,48,2304]{2,1,0:T(8,128)}, u32[]{:S(2)}) copy-start(f32[1,48,2304]{2,1,0:T(8,128)} %core_ref.1) | copy-start | bytes 1327108
  79.4 8.4 %collective-permute-start.1 = (f32[21,2304]{1,0:T(8,128)S(1)}, f32[21,2304]{1,0:T(8,128)S(1)}, u32[]{:S(2)}, u32[]{:S(2)}) collective-permute-start(f32[21,2304]{1,0:T(8,128)S(1)} %pad_maximum_fusion), channel_id=1, source_target_pairs={{32,0},{64,32},{96,64},{128,96},{160,128},{192,160},{224,192},{256... | collective-permute-start | bytes 580616 | tf_op jit(solution)/shard_map/ppermute | solution.py:386
  96.0 16.5 %collective-permute-start.2 = (f32[16,2304]{1,0:T(8,128)S(1)}, f32[16,2304]{1,0:T(8,128)S(1)}, u32[]{:S(2)}, u32[]{:S(2)}) collective-permute-start(f32[16,2304]{1,0:T(8,128)S(1)} %get-tuple-element.16), channel_id=1, source_target_pairs={{0,32},{32,64},{64,96},{96,128},{128,160},{160,192},{192,224},{224... | collective-permute-start | bytes 442376 | tf_op jit(solution)/shard_map/ppermute | solution.py:399
  97.9 14.6 %collective-permute-start.3 = (f32[16,2304]{1,0:T(8,128)S(1)}, f32[16,2304]{1,0:T(8,128)S(1)}, u32[]{:S(2)}, u32[]{:S(2)}) collective-permute-start(f32[16,2304]{1,0:T(8,128)S(1)} %get-tuple-element.17), channel_id=1, source_target_pairs={{32,0},{64,32},{96,64},{128,96},{160,128},{192,160},{224,192},{256... | collective-permute-start | bytes 442376 | tf_op jit(solution)/shard_map/ppermute | solution.py:400

commit v3 on v2

--- a/solution.py
+++ b/solution.py
@@ -21,9 +21,10 @@
 PAD = 8
 SHIFT = 12
 UP = 20
-BLOCK = 384
-BLOCKS = CELLS // BLOCK
-DEPTH = BLOCK + LANES
+PERIOD = 768
+GROUPS = CELLS // PERIOD
+WIDTH = 256
+DEPTH = WIDTH + 2 * LANES
 TILE = 16
 
 EXCHANGE_FACTOR = (3.0 / 3.141592653589793) ** (1.0 / 3.0)
@@ -36,18 +37,15 @@
 
 
 def neighbour_matrix():
-    rows = np.arange(DEPTH)[:, None]
-    cols = np.arange(BLOCK)[None, :]
-    edge = rows - BLOCK
-    after = edge < SIDE
-    before = edge >= LANES - SIDE
-    row_y = np.where(rows < BLOCK, rows // SIDE, np.where(after, BLOCK // SIDE, np.where(before, -1, -9)))
-    row_x = np.where(rows < BLOCK, rows % SIDE, np.where(after, edge, edge - (LANES - SIDE)))
-    gap_x = np.abs(row_x - cols % SIDE)
-    along = (row_y == cols // SIDE) & ((gap_x == 1) | (gap_x == SIDE - 1))
-    across = (gap_x == 0) & (np.abs(row_y - cols // SIDE) == 1)
-    ones = (along | across).astype(ml_dtypes.bfloat16)
-    return np.concatenate([ones, ones], axis=0)
+    parts = []
+    for r in range(PERIOD // WIDTH):
+        rows = (WIDTH * r - LANES + np.arange(DEPTH))[:, None]
+        cols = (WIDTH * r + np.arange(WIDTH))[None, :]
+        gap_x = np.abs(rows % SIDE - cols % SIDE)
+        gap_y = np.abs(rows // SIDE - cols // SIDE)
+        along = (gap_y == 0) & ((gap_x == 1) | (gap_x == SIDE - 1))
+        parts.append((along | ((gap_x == 0) & (gap_y == 1))).astype(ml_dtypes.bfloat16))
+    return np.stack(parts)
 
 
 def tile_of(ref, start):
@@ -59,31 +57,32 @@
         ref[pl.ds(start, 8), pl.ds(LANES * i, LANES)] = pieces[i]
 
 
-def put_split(split_ref, planes, start, upper, lower):
-    lane = lax.broadcasted_iota(jnp.int32, (TILE, LANES), 1)
+def put_split(split_ref, start, upper, lower):
     both = [jnp.concatenate([upper[i], lower[i]], axis=0) for i in range(COLS)]
     high = [x.astype(jnp.bfloat16) for x in both]
     low = [(both[i] - high[i].astype(jnp.float32)).astype(jnp.bfloat16) for i in range(COLS)]
-    for b in range(BLOCKS):
-        rows = pl.ds(b * planes + start, TILE)
+    span = PERIOD // LANES
+    for g in range(GROUPS):
         for k, half in enumerate((high, low)):
-            base = k * DEPTH
-            for j in range(3):
-                split_ref[rows, pl.ds(base + LANES * j, LANES)] = half[3 * b + j]
-            edge = jnp.where(lane < SIDE, half[(3 * b + 3) % COLS], half[(3 * b - 1) % COLS])
-            split_ref[rows, pl.ds(base + BLOCK, LANES)] = edge
-
-
-def multiply(split_ref, matrix_ref, sum_ref, rows):
-    sum_ref[0:rows, :] = jnp.dot(
-        split_ref[0:rows, :], matrix_ref[...], preferred_element_type=jnp.float32
-    )
-
-
-def sum_tile(sum_ref, planes, start):
-    return [
-        sum_ref[pl.ds((i // 3) * planes + start, 8), pl.ds(LANES * (i % 3), LANES)] for i in range(COLS)
-    ]
+            rows = pl.ds((2 * g + k) * BOX + start, TILE)
+            for j in range(span + 2):
+                split_ref[rows, pl.ds(LANES * j, LANES)] = half[(span * g + j - 1) % COLS]
+
+
+def multiply(split_ref, matrix_ref, sum_ref):
+    for r in range(PERIOD // WIDTH):
+        sum_ref[:, WIDTH * r : WIDTH * (r + 1)] = jnp.dot(
+            split_ref[:, WIDTH * r : WIDTH * r + DEPTH], matrix_ref[r], preferred_element_type=jnp.float32
+        )
+
+
+def sum_tile(sum_ref, start):
+    span = PERIOD // LANES
+
+    def part(k, i):
+        return sum_ref[pl.ds((2 * (i // span) + k) * BOX + start, 8), pl.ds(LANES * (i % span), LANES)]
+
+    return [part(0, i) + part(1, i) for i in range(COLS)]
 
 
 def around(flat, before, here, after):
@@ -105,7 +104,7 @@
 
 def split_all(source, split_ref, planes):
     for s in range(0, planes, TILE):
-        put_split(split_ref, planes, s, tile_of(source, PAD + s), tile_of(source, PAD + s + 8))
+        put_split(split_ref, s, tile_of(source, PAD + s), tile_of(source, PAD + s + 8))
 
 
 def update(source, target, split_ref, sum_ref, planes, rule):
@@ -113,11 +112,11 @@
         tiles = [tile_of(source, PAD + s + 8 * k) for k in range(-1, 3)]
         new = []
         for k in range(2):
-            total = around(sum_tile(sum_ref, planes, s + 8 * k), *tiles[k : k + 3])
+            total = around(sum_tile(sum_ref, s + 8 * k), *tiles[k : k + 3])
             new.append(rule(s + 8 * k, tiles[k + 1], total))
             put_tile(target, PAD + s + 8 * k, new[k])
         if split_ref is not None:
-            put_split(split_ref, planes, s, *new)
+            put_split(split_ref, s, *new)
 
 
 def scaled_potential(v_tile, w_ref):
@@ -157,7 +156,7 @@
 
     def step(source, target, rules, last=False):
         for q in range(orbs):
-            multiply(splits[q], matrix_ref, sums[q], BLOCKS * BOX)
+            multiply(splits[q], matrix_ref, sums[q])
         for q in range(orbs):
             update(source[q], target[q], None if last else splits[q], sums[q], BOX, rules(q))
 
@@ -186,14 +185,25 @@
     return out
 
 
-def density_tile(a_refs, scale, factor_ref, core_ref, weight_ref, t, share, psi_out):
-    weight = jnp.broadcast_to(weight_ref[8 * t : 8 * t + 8, :], (8, LANES))
+def occupation_factors(rank_ref, count_ref, occupation_ref, orbs, total):
+    rank = rank_ref[0] * orbs
+    return [
+        jnp.where(rank + q < count_ref[0], occupation_ref[0, q], jnp.float32(0.0)) * (1.0 / total)
+        for q in range(orbs)
+    ]
+
+
+def density_tile(a_refs, scale, factor, core_ref, weight_ref, t, share, psi_out):
+    row = lax.broadcasted_iota(jnp.int32, (8, BOX), 0)
+    column = lax.broadcasted_iota(jnp.int32, (8, BOX), 1)
+    weight = jnp.where(column == row + 8 * t, jnp.broadcast_to(weight_ref[...], (8, BOX)), 0.0)
+    weight = jnp.broadcast_to(jnp.sum(weight, axis=1, keepdims=True), (8, LANES))
     total = [share * c for c in tile_of(core_ref, 8 * t)]
     for q, ref in enumerate(a_refs):
         y = [p * scale[q] for p in tile_of(ref, PAD + 8 * t)]
         if psi_out is not None:
             put_tile(psi_out.at[q], 8 * t, y)
-        total = [total[i] + factor_ref[q] * (y[i] * y[i]) for i in range(COLS)]
+        total = [total[i] + factor[q] * (y[i] * y[i]) for i in range(COLS)]
     return [weight * d for d in total]
 
 
@@ -209,7 +219,7 @@
         return [KEEP * here[i] + SPREAD * total[i] + SOURCE * push[i] for i in range(COLS)]
 
     def one(source, target, last=False):
-        multiply(split_ref, matrix_ref, sum_ref, BLOCKS * BOX)
+        multiply(split_ref, matrix_ref, sum_ref)
         update(source, target, None if last else split_ref, sum_ref, BOX, rule)
 
     split_all(g_ref, split_ref, BOX)
@@ -219,7 +229,7 @@
 
 
 def first_filter(
-    share, factor_ref, orbitals_ref, ext_ref, core_ref, matrix_hbm, weight_ref, guess_ref,
+    orb_count, rank_ref, count_ref, occupation_ref, orbitals_ref, ext_ref, core_ref, matrix_hbm, weight_ref, guess_ref,
     psi_out, density_out, up_out,
     a0, a1, b0, b1, x0, x1, s0, s1, w_ref, matrix_ref, v_ref, c_ref, sem,
 ):
@@ -239,9 +249,10 @@
         copy.wait()
     run_filter((a0, a1), (b0, b1), (x0, x1), (s0, s1), matrix_ref, w_ref, single)
     scale = norms((a0, a1))
+    factor = occupation_factors(rank_ref, count_ref, occupation_ref, 2, 2 * orb_count)
     copies[4].wait()
     for t in range(BOX // 8):
-        put_tile(density_out, 8 * t, density_tile((a0, a1), scale, factor_ref, c_ref, weight_ref, t, share, psi_out))
+        put_tile(density_out, 8 * t, density_tile((a0, a1), scale, factor, c_ref, weight_ref, t, 1.0 / orb_count, psi_out))
     up_out[0:1, :] = guess_ref[...]
     up_out[1:24, :] = density_out[25:48, :]
 
@@ -272,7 +283,7 @@
 
 
 def second_filter(
-    share, factor_ref, psi_ref, ext_ref, core_ref, weight_ref, low_ref, high_ref, owned_ref, matrix_ref,
+    orb_count, rank_ref, count_ref, occupation_ref, psi_ref, ext_ref, core_ref, weight_ref, low_ref, high_ref, owned_ref, matrix_ref,
     density_out, up_out, down_out, charge_out,
     a0, a1, b0, b1, x0, x1, s0, s1, w_ref, v_ref,
 ):
@@ -289,9 +300,10 @@
     single = scaled_potential(lambda r: tile_of(v_ref, r), w_ref)
     run_filter((a0, a1), (b0, b1), (x0, x1), (s0, s1), matrix_ref, w_ref, single)
     scale = norms((a0, a1))
+    factor = occupation_factors(rank_ref, count_ref, occupation_ref, 2, 2 * orb_count)
     charge = [jnp.zeros((8, LANES), jnp.float32) for _ in range(3)]
     for t in range(BOX // 8):
-        tile = density_tile((a0, a1), scale, factor_ref, core_ref, weight_ref, t, share, None)
+        tile = density_tile((a0, a1), scale, factor, core_ref, weight_ref, t, 1.0 / orb_count, None)
         put_tile(density_out, 8 * t, tile)
         for i, d in enumerate(tile):
             charge[i % 3] = charge[i % 3] + d
@@ -330,6 +342,7 @@
 SMEM = pl.BlockSpec(memory_space=pltpu.SMEM)
 HBM = pl.BlockSpec(memory_space=pltpu.HBM)
 LIMIT = pltpu.CompilerParams(vmem_limit_bytes=48 * 2**20)
+FIRST = 62 * 2**20
 
 
 def f32(*shape):
@@ -341,31 +354,27 @@
     dom_count = lax.axis_size("dom")
     orb_rank = lax.axis_index("orb")
     per_device = orbitals.shape[1]
-    rank = orb_rank * per_device + jnp.arange(per_device, dtype=jnp.int32)
-    factors = jnp.where(rank < occupied_count[0], occupations[0], jnp.float32(0.0)) / (per_device * orb_count)
-    weight = weights.reshape(BOX, 1)
     place = orb_rank.reshape(1)
-    share = 1.0 / orb_count
     up = [(i, (i + 1) % dom_count) for i in range(dom_count)]
     down = [(j, i) for i, j in up]
     matrix = jnp.asarray(neighbour_matrix())
     padded = pltpu.VMEM((BOX + 2 * PAD, CELLS), jnp.float32)
-    split = pltpu.VMEM((BLOCKS * BOX, 2 * DEPTH), jnp.bfloat16)
-    sums = pltpu.VMEM((BLOCKS * BOX, BLOCK), jnp.float32)
+    split = pltpu.VMEM((2 * GROUPS * BOX, PERIOD + 2 * LANES), jnp.bfloat16)
+    sums = pltpu.VMEM((2 * GROUPS * BOX, PERIOD), jnp.float32)
     box = pltpu.VMEM((BOX, CELLS), jnp.float32)
-    whole = pltpu.VMEM((2 * DEPTH, BLOCK), jnp.bfloat16)
+    whole = pltpu.VMEM((PERIOD // WIDTH, DEPTH, WIDTH), jnp.bfloat16)
     filter_scratch = [padded] * 4 + [split] * 2 + [sums] * 2 + [box]
     relax_scratch = [padded, padded, box, split, sums]
 
     psi, density, upper = pl.pallas_call(
-        functools.partial(first_filter, share),
-        in_specs=[SMEM] + [HBM] * 4 + [VMEM] * 2,
+        functools.partial(first_filter, orb_count),
+        in_specs=[SMEM] * 3 + [HBM] * 4 + [VMEM] * 2,
         out_specs=[VMEM] * 3,
         out_shape=[f32(per_device, BOX, CELLS), f32(BOX, CELLS), f32(24, CELLS)],
         scratch_shapes=filter_scratch + [whole, box, box, pltpu.SemaphoreType.DMA((5,))],
-        compiler_params=LIMIT,
+        compiler_params=pltpu.CompilerParams(vmem_limit_bytes=FIRST),
         name="first_filter",
-    )(factors, orbitals, external_potential, core_density, matrix, weight, hartree_guess)
+    )(place, occupied_count, occupations, orbitals, external_potential, core_density, matrix, weights, hartree_guess)
 
     behind = lax.ppermute(upper, "dom", up)
     sent = pl.pallas_call(
@@ -386,14 +395,17 @@
     high = lax.ppermute(jnp.concatenate([low[:UP], owned_hartree], axis=0), "dom", down)
 
     density, upper, lower, charge = pl.pallas_call(
-        functools.partial(second_filter, share),
-        in_specs=[SMEM] + [VMEM] * 8,
+        functools.partial(second_filter, orb_count),
+        in_specs=[SMEM] * 3 + [VMEM] * 8,
         out_specs=[VMEM] * 4,
         out_shape=[f32(BOX, CELLS), f32(16, CELLS), f32(16, CELLS), f32(dom_count, 1, LANES)],
         scratch_shapes=filter_scratch + [box],
         compiler_params=LIMIT,
         name="second_filter",
-    )(factors, psi, external_potential[0], core_density[0], weight, low, high, owned_density, matrix)
+    )(
+        place, occupied_count, occupations, psi, external_potential[0], core_density[0], weights, low, high,
+        owned_density, matrix,
+    )
 
     charge = lax.all_to_all(charge, "dom", 0, 0, tiled=True).sum(axis=0)
     from_below = lax.ppermute(upper, "dom", up)

time: 145 us -> 141 us (0.972)
  the two profiles are of different devices: /device:TPU:64 before, /device:TPU:2 now
where the time goes in v3:
time: 141 us; the launch traced here: 140 us
  blocking collectives  92.3 us (65%)
  Pallas kernels  21.2 us (15%)
  starting transfers between devices  11.3 us (8%)
  waiting for transfers between devices  9.84 us (7%)
  local copies, waits for them, and re-layouts  2.45 us (2%)
  other arithmetic  1.52 us (1%)
  between operations  1.48 us (1%)
    all_to_all x2, blocking collectives, body(): total = lax.all_to_all(sent, 'orb', 0, 0, tiled=True).sum(axis=0)  58.7 us
    all_to_all x1, blocking collectives, body(): lax.all_to_all(jnp.broadcast_to(plane[None], (orb_count, 1, CELLS)), 'orb...  21.2 us
    all_to_all x1, blocking collectives, body(): charge = lax.all_to_all(charge, 'dom', 0, 0, tiled=True).sum(axis=0)  12.4 us
    pallas_call x1, Pallas kernels, body(): pl.pallas_call(functools.partial(first_filter, orb_count), in_specs=[SMEM...  9.97 us
    pallas_call x1, Pallas kernels, body(): pl.pallas_call(functools.partial(second_filter, orb_count), in_specs=[SME...  7.19 us
    ppermute x1, waiting for transfers between devices, body(): behind = lax.ppermute(upper, 'dom', up)  6.43 us
    ppermute x1, starting transfers between devices, body(): from_below = lax.ppermute(upper, 'dom', up)  5.39 us
    ppermute x1, waiting for transfers between devices, body(): lax.ppermute(jnp.concatenate([low[:UP], owned_hartree], axis=0), 'dom', d...  3.4 us
  transfers between devices with their start and end apart: 4, of which 2 were waited for; matrix products, arithmetic and copies ran while one was open for 0% of the time, Pallas kernels for 0%

profile of v3, /device:TPU:2, one launch (start us, length us, event | category | flops | bytes accessed | tf_op | source)
XLA Modules:
  0.0 140.1 jit_solution(14485096983086539395)
XLA Ops:
  0.7 0.0 copy-start
  0.7 0.0 copy-start.5
  0.7 10.0 %first_filter.1 = (f32[2,48,2304]{2,1,0:T(8,128)}, f32[48,2304]{1,0:T(8,128)}, f32[24,2304]{1,0:T(8,128)}) custom-call(s32[1]{0:T(128)} %bitcast.rank_ref, s32[1]{0:T(128)S(6)} %copy.16.count_ref, f32[1,2]{1,0:T(1,128)} %occupation_ref.3, f32[1,2,48,2304]{3,2,1,0:T(8,128)} %orbitals_ref.1, f32[1,48,2304]{2,1,0:T(8,128)} %ext_ref.1, f32[1,48,2304]{2,1,0:T(8,128)} %core_ref.1, ...), custom_call_target="tpu_custom_call" | custom-call | tf_op jit(solution)/shard_map/first_filter/pallas_call | solution.py:369
  10.7 1.9 %collective-permute-start = (f32[24,2304]{1,0:T(8,128)}, f32[24,2304]{1,0:T(8,128)S(1)}, u32[]{:S(2)}, u32[]{:S(2)}) collective-permute-start(f32[24,2304]{1,0:T(8,128)} %get-tuple-element.14), channel_id=1, source_target_pairs={{0,32},{32,64},{64,96},{96,128},{128,160},{160,192},{192,224},{224... | collective-permute-start | bytes 663560 | tf_op jit(solution)/shard_map/ppermute | solution.py:379
  12.6 6.4 %collective-permute-done.behind_ref = f32[24,2304]{1,0:T(8,128)S(1)} collective-permute-done((f32[24,2304]{1,0:T(8,128)}, f32[24,2304]{1,0:T(8,128)S(1)}, u32[]{:S(2)}, u32[]{:S(2)}) %collective-permute-start) | collective-permute-done | bytes 221216 | tf_op jit(solution)/shard_map/ppermute | solution.py:379
  19.0 0.0 copy-done
  19.0 0.0 copy-done.5
  19.0 0.0 copy-start.4
  19.0 1.0 copy-done.4
  20.0 1.9 %first_relax.1 = f32[32,1,4608]{2,1,0:T(1,128)S(1)} custom-call(s32[1]{0:T(128)} %bitcast.rank_ref, f32[48,2304]{1,0:T(8,128)S(1)} %copy-done.4, f32[24,2304]{1,0:T(8,128)S(1)} %collective-permute-done.behind_ref, f32[1,2304]{1,0:T(1,128)S(1)} %copy-done.5, bf16[3,512,256]{2,1,0:T(8,128)(2,1)S(1)} %copy-done), custom_call_target="tpu_custom_call" | custom-call | tf_op jit(solution)/shard_map/first_relax/pallas_call | solution.py:380
  21.9 32.0 %all_to_all.20 = f32[32,1,4608]{2,1,0:T(1,128)S(1)} all-to-all(f32[32,1,4608]{2,1,0:T(1,128)S(1)} %first_relax.1), channel_id=1, replica_groups=mesh['dom'=16,'orb'=32] {'orb'}, dimensions={0} | all-to-all | bytes 1179648 | tf_op jit(solution)/shard_map/all_to_all | solution.py:389
  53.9 0.3 reduce_sum.33
  54.3 0.1 fusion.2
  54.4 0.2 broadcast_in_dim.9
  54.5 21.2 %all_to_all.21 = f32[32,1,2304]{2,1,0:T(1,128)S(1)} all-to-all(f32[32,1,2304]{2,1,0:T(1,128)S(1)} %broadcast_in_dim.9), channel_id=1, replica_groups=mesh['dom'=16,'orb'=32] {'orb'}, dimensions={0} | all-to-all | bytes 589824 | tf_op jit(solution)/shard_map/all_to_all | solution.py:393
  75.7 0.0 copy-start.3
  75.8 0.0 copy-start.1
  75.8 0.0 copy-start.2
  75.9 2.1 %collective-permute-start.1 = (f32[21,2304]{1,0:T(8,128)S(1)}, f32[21,2304]{1,0:T(8,128)S(1)}, u32[]{:S(2)}, u32[]{:S(2)}) collective-permute-start(f32[21,2304]{1,0:T(8,128)S(1)} %pad_maximum_fusion), channel_id=1, source_target_pairs={{32,0},{64,32},{96,64},{128,96},{160,128},{192,160},{224,192},{256... | collective-permute-start | bytes 580616 | tf_op jit(solution)/shard_map/ppermute | solution.py:395
  77.9 3.4 %collective-permute-done.1.high_ref = f32[21,2304]{1,0:T(8,128)S(1)} collective-permute-done((f32[21,2304]{1,0:T(8,128)S(1)}, f32[21,2304]{1,0:T(8,128)S(1)}, u32[]{:S(2)}, u32[]{:S(2)}) %collective-permute-start.1) | collective-permute-done | bytes 193568 | tf_op jit(solution)/shard_map/ppermute | solution.py:395
  81.3 0.0 copy-start.6
  81.3 0.0 copy-start.7
  81.3 0.0 copy-done.3
  81.3 0.0 copy-done.1
  81.4 0.0 copy-done.2
  81.4 0.6 copy-done.6
  82.0 0.0 copy-done.7
  82.0 7.2 %second_filter.1 = (f32[48,2304]{1,0:T(8,128)S(1)}, f32[16,2304]{1,0:T(8,128)S(1)}, f32[16,2304]{1,0:T(8,128)S(1)}, f32[16,1,128]{2,1,0:T(1,128)S(1)}) custom-call(s32[1]{0:T(128)} %bitcast.rank_ref, s32[1]{0:T(128)S(6)} %copy.16.count_ref, f32[1,2]{1,0:T(1,128)S(1)} %copy-done.6, f32[2,48,2304]{2,1,0:T(8,128)S(1)} %copy-done.3, f32[48,2304]{1,0:T(8,128)S(1)} %bitcast.11, ...), custom_call_target="tpu_custom_call" | custom-call | tf_op jit(solution)/shard_map/second_filter/pallas_call | solution.py:397
  89.2 5.4 %collective-permute-start.2 = (f32[16,2304]{1,0:T(8,128)S(1)}, f32[16,2304]{1,0:T(8,128)S(1)}, u32[]{:S(2)}, u32[]{:S(2)}) collective-permute-start(f32[16,2304]{1,0:T(8,128)S(1)} %get-tuple-element.16), channel_id=1, source_target_pairs={{0,32},{32,64},{64,96},{96,128},{128,160},{160,192},{192,224},{224... | collective-permute-start | bytes 442376 | tf_op jit(solution)/shard_map/ppermute | solution.py:411
  94.6 1.9 %collective-permute-start.3 = (f32[16,2304]{1,0:T(8,128)S(1)}, f32[16,2304]{1,0:T(8,128)S(1)}, u32[]{:S(2)}, u32[]{:S(2)}) collective-permute-start(f32[16,2304]{1,0:T(8,128)S(1)} %get-tuple-element.17), channel_id=1, source_target_pairs={{32,0},{64,32},{96,64},{128,96},{160,128},{192,160},{224,192},{256... | collective-permute-start | bytes 442376 | tf_op jit(solution)/shard_map/ppermute | solution.py:412
  96.5 12.4 %all_to_all.22 = f32[16,1,128]{2,1,0:T(1,128)S(1)} all-to-all(f32[16,1,128]{2,1,0:T(1,128)S(1)} %get-tuple-element.18), channel_id=1, replica_groups=mesh['dom'=16,'orb'=32] {'dom'}, dimensions={0} | all-to-all | bytes 16384 | tf_op jit(solution)/shard_map/all_to_all | solution.py:410
  109.0 0.0 collective-permute-done.2.below_ref
  109.0 0.0 collective-permute-done.3.above_ref
  109.0 2.1 %second_relax.1 = f32[32,1,4736]{2,1,0:T(1,128)S(1)} custom-call(s32[1]{0:T(128)} %bitcast.rank_ref, f32[48,2304]{1,0:T(8,128)S(1)} %get-tuple-element.15.density_ref, f32[16,2304]{1,0:T(8,128)S(1)} %collective-permute-done.2.below_ref, f32[16,2304]{1,0:T(8,128)S(1)} %collective-permute-done.3.above_ref, f32[1,2304]{1,0:T(1,128)S(1)} %get-tuple-element.21.plane_ref, ...), custom_call_target="tpu_custom_call" | custom-call | tf_op jit(solution)/shard_map/second_relax/pallas_call | solution.py:413
  111.1 26.7 %all_to_all.23 = f32[32,1,4736]{2,1,0:T(1,128)S(1)} all-to-all(f32[32,1,4736]{2,1,0:T(1,128)S(1)} %second_relax.1), channel_id=1, replica_groups=mesh['dom'=16,'orb'=32] {'orb'}, dimensions={0} | all-to-all | bytes 1212416 | tf_op jit(solution)/shard_map/all_to_all | solution.py:422
  137.8 0.3 reduce_sum.37
  138.2 0.5 slice.32
  139.4 0.7 fusion.1
  (7 shorter events, 0.2 us)
Async XLA Ops:
  0.7 18.4 %copy-start = (bf16[3,512,256]{2,1,0:T(8,128)(2,1)S(1)}, bf16[3,512,256]{2,1,0:T(8,128)(2,1)}, u32[]{:S(2)}) copy-start(bf16[3,512,256]{2,1,0:T(8,128)(2,1)} %constant.15.clone.matrix_hbm.matrix_ref) | copy-start | bytes 2359300
  0.7 18.4 %copy-start.5 = (f32[1,2304]{1,0:T(1,128)S(1)}, f32[1,2304]{1,0:T(1,128)}, u32[]{:S(2)}) copy-start(f32[1,2304]{1,0:T(1,128)} %guess_ref.3) | copy-start | bytes 27652
  10.7 8.4 %collective-permute-start = (f32[24,2304]{1,0:T(8,128)}, f32[24,2304]{1,0:T(8,128)S(1)}, u32[]{:S(2)}, u32[]{:S(2)}) collective-permute-start(f32[24,2304]{1,0:T(8,128)} %get-tuple-element.14), channel_id=1, source_target_pairs={{0,32},{32,64},{64,96},{96,128},{128,160},{160,192},{192,224},{224... | collective-permute-start | bytes 663560 | tf_op jit(solution)/shard_map/ppermute | solution.py:379
  19.0 1.0 copy-start.4
  75.7 5.6 %copy-start.3 = (f32[2,48,2304]{2,1,0:T(8,128)S(1)}, f32[2,48,2304]{2,1,0:T(8,128)}, u32[]{:S(2)}) copy-start(f32[2,48,2304]{2,1,0:T(8,128)} %get-tuple-element.12.psi_ref) | copy-start | bytes 2654212
  75.8 5.6 %copy-start.1 = (f32[1,48,2304]{2,1,0:T(8,128)S(1)}, f32[1,48,2304]{2,1,0:T(8,128)}, u32[]{:S(2)}) copy-start(f32[1,48,2304]{2,1,0:T(8,128)} %ext_ref.1) | copy-start | bytes 1327108
  75.8 5.5 %copy-start.2 = (f32[1,48,2304]{2,1,0:T(8,128)S(1)}, f32[1,48,2304]{2,1,0:T(8,128)}, u32[]{:S(2)}) copy-start(f32[1,48,2304]{2,1,0:T(8,128)} %core_ref.1) | copy-start | bytes 1327108
  75.9 5.5 %collective-permute-start.1 = (f32[21,2304]{1,0:T(8,128)S(1)}, f32[21,2304]{1,0:T(8,128)S(1)}, u32[]{:S(2)}, u32[]{:S(2)}) collective-permute-start(f32[21,2304]{1,0:T(8,128)S(1)} %pad_maximum_fusion), channel_id=1, source_target_pairs={{32,0},{64,32},{96,64},{128,96},{160,128},{192,160},{224,192},{256... | collective-permute-start | bytes 580616 | tf_op jit(solution)/shard_map/ppermute | solution.py:395
  81.3 0.7 copy-start.6
  81.3 0.7 copy-start.7
  89.2 19.8 %collective-permute-start.2 = (f32[16,2304]{1,0:T(8,128)S(1)}, f32[16,2304]{1,0:T(8,128)S(1)}, u32[]{:S(2)}, u32[]{:S(2)}) collective-permute-start(f32[16,2304]{1,0:T(8,128)S(1)} %get-tuple-element.16), channel_id=1, source_target_pairs={{0,32},{32,64},{64,96},{96,128},{128,160},{160,192},{192,224},{224... | collective-permute-start | bytes 442376 | tf_op jit(solution)/shard_map/ppermute | solution.py:411
  94.6 14.4 %collective-permute-start.3 = (f32[16,2304]{1,0:T(8,128)S(1)}, f32[16,2304]{1,0:T(8,128)S(1)}, u32[]{:S(2)}, u32[]{:S(2)}) collective-permute-start(f32[16,2304]{1,0:T(8,128)S(1)} %get-tuple-element.17), channel_id=1, source_target_pairs={{32,0},{64,32},{96,64},{128,96},{160,128},{192,160},{224,192},{256... | collective-permute-start | bytes 442376 | tf_op jit(solution)/shard_map/ppermute | solution.py:412

commit v4 on v3

--- a/solution.py
+++ b/solution.py
@@ -69,8 +69,8 @@
                 split_ref[rows, pl.ds(LANES * j, LANES)] = half[(span * g + j - 1) % COLS]
 
 
-def multiply(split_ref, matrix_ref, sum_ref):
-    for r in range(PERIOD // WIDTH):
+def multiply(split_ref, matrix_ref, sum_ref, parts=range(PERIOD // WIDTH)):
+    for r in parts:
         sum_ref[:, WIDTH * r : WIDTH * (r + 1)] = jnp.dot(
             split_ref[:, WIDTH * r : WIDTH * r + DEPTH], matrix_ref[r], preferred_element_type=jnp.float32
         )
@@ -102,19 +102,21 @@
         ref[PAD + planes : 2 * PAD + planes, :] = zero
 
 
-def split_all(source, split_ref, planes):
-    for s in range(0, planes, TILE):
+def split_all(source, split_ref):
+    for s in range(0, BOX, TILE):
         put_split(split_ref, s, tile_of(source, PAD + s), tile_of(source, PAD + s + 8))
 
 
-def update(source, target, split_ref, sum_ref, planes, rule):
-    for s in range(0, planes, TILE):
-        tiles = [tile_of(source, PAD + s + 8 * k) for k in range(-1, 3)]
+def update(source, target, split_ref, sum_ref, rule, beside=None):
+    for k, s in enumerate(range(0, BOX, TILE)):
+        if beside is not None:
+            beside(k)
+        tiles = [tile_of(source, PAD + s + 8 * n) for n in range(-1, 3)]
         new = []
-        for k in range(2):
-            total = around(sum_tile(sum_ref, s + 8 * k), *tiles[k : k + 3])
-            new.append(rule(s + 8 * k, tiles[k + 1], total))
-            put_tile(target, PAD + s + 8 * k, new[k])
+        for n in range(2):
+            total = around(sum_tile(sum_ref, s + 8 * n), *tiles[n : n + 3])
+            new.append(rule(s + 8 * n, tiles[n + 1], total))
+            put_tile(target, PAD + s + 8 * n, new[n])
         if split_ref is not None:
             put_split(split_ref, s, *new)
 
@@ -156,12 +158,19 @@
 
     def step(source, target, rules, last=False):
         for q in range(orbs):
-            multiply(splits[q], matrix_ref, sums[q])
-        for q in range(orbs):
-            update(source[q], target[q], None if last else splits[q], sums[q], BOX, rules(q))
+            after = (q + 1) % orbs
+
+            def beside(k):
+                multiply(splits[after], matrix_ref, sums[after], [k])
+
+            update(
+                source[q], target[q], None if last else splits[q], sums[q], rules(q),
+                None if last and after == 0 else beside,
+            )
 
     for q in range(orbs):
-        split_all(a_refs[q], splits[q], BOX)
+        split_all(a_refs[q], splits[q])
+    multiply(splits[0], matrix_ref, sums[0])
     step(a_refs, b_refs, first_rule)
 
     def pair(k, carry):
@@ -193,7 +202,7 @@
     ]
 
 
-def density_tile(a_refs, scale, factor, core_ref, weight_ref, t, share, psi_out):
+def density_tile(a_refs, scale, factor, core_ref, weight_ref, t, share):
     row = lax.broadcasted_iota(jnp.int32, (8, BOX), 0)
     column = lax.broadcasted_iota(jnp.int32, (8, BOX), 1)
     weight = jnp.where(column == row + 8 * t, jnp.broadcast_to(weight_ref[...], (8, BOX)), 0.0)
@@ -201,8 +210,6 @@
     total = [share * c for c in tile_of(core_ref, 8 * t)]
     for q, ref in enumerate(a_refs):
         y = [p * scale[q] for p in tile_of(ref, PAD + 8 * t)]
-        if psi_out is not None:
-            put_tile(psi_out.at[q], 8 * t, y)
         total = [total[i] + factor[q] * (y[i] * y[i]) for i in range(COLS)]
     return [weight * d for d in total]
 
@@ -220,9 +227,9 @@
 
     def one(source, target, last=False):
         multiply(split_ref, matrix_ref, sum_ref)
-        update(source, target, None if last else split_ref, sum_ref, BOX, rule)
-
-    split_all(g_ref, split_ref, BOX)
+        update(source, target, None if last else split_ref, sum_ref, rule)
+
+    split_all(g_ref, split_ref)
     for k in range(SWEEPS // 2):
         one(g_ref, h_ref)
         one(h_ref, g_ref, last=k == SWEEPS // 2 - 1)
@@ -231,30 +238,55 @@
 def first_filter(
     orb_count, rank_ref, count_ref, occupation_ref, orbitals_ref, ext_ref, core_ref, matrix_hbm, weight_ref, guess_ref,
     psi_out, density_out, up_out,
-    a0, a1, b0, b1, x0, x1, s0, s1, w_ref, matrix_ref, v_ref, c_ref, sem,
+    a0, a1, b0, b1, x0, x1, s0, s1, w_ref, matrix_ref, v_ref, c_ref, scale_ref, sem,
 ):
-    copies = [
-        pltpu.make_async_copy(ext_ref.at[0], v_ref, sem.at[0]),
-        pltpu.make_async_copy(orbitals_ref.at[0, 0], a0.at[PAD : PAD + BOX], sem.at[1]),
-        pltpu.make_async_copy(orbitals_ref.at[0, 1], a1.at[PAD : PAD + BOX], sem.at[2]),
-        pltpu.make_async_copy(matrix_hbm, matrix_ref, sem.at[3]),
-        pltpu.make_async_copy(core_ref.at[0], c_ref, sem.at[4]),
+    third = BOX // 3
+    copies = []
+    for n, (source, target, first) in enumerate((
+        (ext_ref.at[0], v_ref, 0), (orbitals_ref.at[0, 0], a0, PAD), (orbitals_ref.at[0, 1], a1, PAD),
+        (core_ref.at[0], c_ref, 0),
+    )):
+        copies.append([
+            pltpu.make_async_copy(
+                source.at[third * k : third * (k + 1)], target.at[first + third * k : first + third * (k + 1)],
+                sem.at[n, k],
+            )
+            for k in range(3)
+        ])
+    copies.append([pltpu.make_async_copy(matrix_hbm.at[k], matrix_ref.at[k], sem.at[4, k]) for k in range(3)])
+    for n in (0, 1, 4, 2, 3):
+        for copy in copies[n]:
+            copy.start()
+
+    def arrived(n):
+        for copy in copies[n]:
+            copy.wait()
+
+    clear_pads((a0, a1, b0, b1), BOX)
+    arrived(0)
+    single = scaled_potential(lambda r: tile_of(v_ref, r), w_ref)
+    for n in (1, 4, 2):
+        arrived(n)
+    run_filter((a0, a1), (b0, b1), (x0, x1), (s0, s1), matrix_ref, w_ref, single)
+    leaving = [
+        pltpu.make_async_copy(ref.at[PAD : PAD + BOX], psi_out.at[q, 0:BOX], sem.at[5, q])
+        for q, ref in enumerate((a0, a1))
     ]
-    for copy in copies:
+    for copy in leaving:
         copy.start()
-    clear_pads((a0, a1, b0, b1), BOX)
-    copies[0].wait()
-    single = scaled_potential(lambda r: tile_of(v_ref, r), w_ref)
-    for copy in copies[1:4]:
-        copy.wait()
-    run_filter((a0, a1), (b0, b1), (x0, x1), (s0, s1), matrix_ref, w_ref, single)
     scale = norms((a0, a1))
+    for q in range(2):
+        put_tile(scale_ref, 8 * q, [scale[q]] * COLS)
+        leaving.append(pltpu.make_async_copy(scale_ref.at[8 * q : 8 * q + 8], psi_out.at[q, BOX : BOX + 8], sem.at[6, q]))
+        leaving[-1].start()
     factor = occupation_factors(rank_ref, count_ref, occupation_ref, 2, 2 * orb_count)
-    copies[4].wait()
-    for t in range(BOX // 8):
-        put_tile(density_out, 8 * t, density_tile((a0, a1), scale, factor, c_ref, weight_ref, t, 1.0 / orb_count, psi_out))
+    arrived(3)
+    for t in range(BOX // 8):
+        put_tile(density_out, 8 * t, density_tile((a0, a1), scale, factor, c_ref, weight_ref, t, 1.0 / orb_count))
     up_out[0:1, :] = guess_ref[...]
     up_out[1:24, :] = density_out[25:48, :]
+    for copy in leaving:
+        copy.wait()
 
 
 def first_relax(rank_ref, density_ref, behind_ref, guess_ref, matrix_ref, out_ref, g_ref, h_ref, d_ref, x0, s0):
@@ -288,8 +320,10 @@
     a0, a1, b0, b1, x0, x1, s0, s1, w_ref, v_ref,
 ):
     clear_pads((a0, a1, b0, b1), BOX)
-    a0[PAD : PAD + BOX, :] = psi_ref[0]
-    a1[PAD : PAD + BOX, :] = psi_ref[1]
+    for q, ref in enumerate((a0, a1)):
+        scale = tile_of(psi_ref.at[q], BOX)[0]
+        for t in range(BOX // 8):
+            put_tile(ref, PAD + 8 * t, [y * scale for y in tile_of(psi_ref.at[q], 8 * t)])
     first = SHIFT - BUF
     v_ref[0 : CORE - first, :] = low_ref[first:CORE, :]
     v_ref[CORE - first : BOX, :] = high_ref[0:UP, :]
@@ -303,7 +337,7 @@
     factor = occupation_factors(rank_ref, count_ref, occupation_ref, 2, 2 * orb_count)
     charge = [jnp.zeros((8, LANES), jnp.float32) for _ in range(3)]
     for t in range(BOX // 8):
-        tile = density_tile((a0, a1), scale, factor, core_ref, weight_ref, t, 1.0 / orb_count, None)
+        tile = density_tile((a0, a1), scale, factor, core_ref, weight_ref, t, 1.0 / orb_count)
         put_tile(density_out, 8 * t, tile)
         for i, d in enumerate(tile):
             charge[i % 3] = charge[i % 3] + d
@@ -338,6 +372,23 @@
         out_ref[p, :, 2 * CELLS : 2 * CELLS + LANES] = charge_ref[...]
 
 
+def keep_kernel(density_ref, weight_ref, occupation_ref, density_out, weight_out, occupation_out):
+    density_out[...] = density_ref[...]
+    weight_out[...] = weight_ref[...]
+    occupation_out[...] = occupation_ref[...]
+
+
+def last_kernel(cells_everywhere, arrived_ref, out_ref):
+    total = [arrived_ref[k] for k in range(4)]
+    for k in range(4, CORE):
+        total[k % 4] = total[k % 4] + arrived_ref[k]
+    total = (total[0] + total[1]) + (total[2] + total[3])
+    density = total[:, :CELLS]
+    average = total[:, 2 * CELLS : 2 * CELLS + 1] * (1.0 / cells_everywhere)
+    exchange = EXCHANGE_FACTOR * jnp.exp(jnp.log(density) * (1.0 / 3.0))
+    out_ref[...] = total[:, CELLS : 2 * CELLS] - (SWEEPS * SOURCE) * average - exchange
+
+
 VMEM = pl.BlockSpec(memory_space=pltpu.VMEM)
 SMEM = pl.BlockSpec(memory_space=pltpu.SMEM)
 HBM = pl.BlockSpec(memory_space=pltpu.HBM)
@@ -369,14 +420,24 @@
     psi, density, upper = pl.pallas_call(
         functools.partial(first_filter, orb_count),
         in_specs=[SMEM] * 3 + [HBM] * 4 + [VMEM] * 2,
-        out_specs=[VMEM] * 3,
-        out_shape=[f32(per_device, BOX, CELLS), f32(BOX, CELLS), f32(24, CELLS)],
-        scratch_shapes=filter_scratch + [whole, box, box, pltpu.SemaphoreType.DMA((5,))],
+        out_specs=[HBM] + [VMEM] * 2,
+        out_shape=[f32(per_device, BOX + 8, CELLS), f32(BOX, CELLS), f32(24, CELLS)],
+        scratch_shapes=filter_scratch
+        + [whole, box, box, pltpu.VMEM((16, CELLS), jnp.float32), pltpu.SemaphoreType.DMA((7, 3))],
         compiler_params=pltpu.CompilerParams(vmem_limit_bytes=FIRST),
         name="first_filter",
     )(place, occupied_count, occupations, orbitals, external_potential, core_density, matrix, weights, hartree_guess)
 
     behind = lax.ppermute(upper, "dom", up)
+    density, near_weights, near_occupations = pl.pallas_call(
+        keep_kernel,
+        in_specs=[VMEM] * 3,
+        out_specs=[VMEM] * 3,
+        out_shape=[f32(BOX, CELLS), f32(1, BOX), f32(1, per_device)],
+        compiler_params=LIMIT,
+        cost_estimate=pl.CostEstimate(flops=10**6, bytes_accessed=4 * 10**6, transcendentals=0),
+        name="keep",
+    )(density, weights, occupations)
     sent = pl.pallas_call(
         first_relax,
         in_specs=[SMEM] + [VMEM] * 4,
@@ -403,7 +464,7 @@
         compiler_params=LIMIT,
         name="second_filter",
     )(
-        place, occupied_count, occupations, psi, external_potential[0], core_density[0], weights, low, high,
+        place, occupied_count, near_occupations, psi, external_potential[0], core_density[0], near_weights, low, high,
         owned_density, matrix,
     )
 
@@ -419,10 +480,15 @@
         compiler_params=LIMIT,
         name="second_relax",
     )(place, density, from_below, from_above, owned_hartree, high, charge, matrix)
-    total = lax.all_to_all(sent, "orb", 0, 0, tiled=True).sum(axis=0)
-    density = total[:, :CELLS]
-    average = total[:, 2 * CELLS : 2 * CELLS + 1] / (dom_count * CORE * CELLS)
-    return total[:, CELLS : 2 * CELLS] - (SWEEPS * SOURCE) * average - EXCHANGE_FACTOR * jnp.cbrt(density)
+    arrived = lax.all_to_all(sent, "orb", 0, 0, tiled=True)
+    return pl.pallas_call(
+        functools.partial(last_kernel, dom_count * CORE * CELLS),
+        in_specs=[VMEM],
+        out_specs=VMEM,
+        out_shape=f32(1, CELLS),
+        compiler_params=LIMIT,
+        name="last",
+    )(arrived)
 
 
 def solution(mesh):

time: 141 us -> 138 us (0.979)
    all_to_all x0 -> x1, blocking collectives: none -> 26.8 us  [body(): arrived = lax.all_to_all(sent, 'orb', 0, 0, tiled=True)]
    all_to_all x2 -> x1, blocking collectives: 58.7 us -> 32 us  [body(): total = lax.all_to_all(sent, 'orb', 0, 0, tiled=True).sum(axis=0)]
where the time goes in v4:
time: 138 us
  blocking collectives  92.5 us (67%)
  Pallas kernels  22.4 us (16%)
  starting transfers between devices  11.3 us (8%)
  waiting for transfers between devices  8.77 us (6%)
    all_to_all x1, blocking collectives, body(): total = lax.all_to_all(sent, 'orb', 0, 0, tiled=True).sum(axis=0)  32 us
    all_to_all x1, blocking collectives, body(): arrived = lax.all_to_all(sent, 'orb', 0, 0, tiled=True)  26.8 us
    all_to_all x1, blocking collectives, body(): lax.all_to_all(jnp.broadcast_to(plane[None], (orb_count, 1, CELLS)), 'orb...  21.3 us
    all_to_all x1, blocking collectives, body(): charge = lax.all_to_all(charge, 'dom', 0, 0, tiled=True).sum(axis=0)  12.4 us
    pallas_call x1, Pallas kernels, body(): pl.pallas_call(functools.partial(first_filter, orb_count), in_specs=[SMEM...  10.5 us
    pallas_call x1, Pallas kernels, body(): pl.pallas_call(functools.partial(second_filter, orb_count), in_specs=[SME...  7.34 us
    ppermute x1, starting transfers between devices, body(): from_below = lax.ppermute(upper, 'dom', up)  5.41 us
    ppermute x1, waiting for transfers between devices, body(): behind = lax.ppermute(upper, 'dom', up)  5.36 us
  transfers between devices with their start and end apart: 4, of which 2 were waited for; matrix products, arithmetic and copies ran while one was open for 0% of the time, Pallas kernels for 0%

profile of v4, /device:TPU:2, one launch (start us, length us, event | category | flops | bytes accessed | tf_op | source)
XLA Modules:
  0.0 137.5 jit_solution(8076664821320412179)
XLA Ops:
  0.7 0.0 copy-start
  0.7 10.5 %first_filter.1 = (f32[2,56,2304]{2,1,0:T(8,128)}, f32[48,2304]{1,0:T(8,128)}, f32[24,2304]{1,0:T(8,128)}) custom-call(s32[1]{0:T(128)} %bitcast.rank_ref, s32[1]{0:T(128)S(6)} %copy.16.count_ref, f32[1,2]{1,0:T(1,128)} %occupation_ref.3, f32[1,2,48,2304]{3,2,1,0:T(8,128)} %orbitals_ref.1, f32[1,48,2304]{2,1,0:T(8,128)} %ext_ref.1, f32[1,48,2304]{2,1,0:T(8,128)} %core_ref.1, ...), custom_call_target="tpu_custom_call" | custom-call | tf_op jit(solution)/shard_map/first_filter/pallas_call | solution.py:420
  11.2 0.0 copy-start.6
  11.2 0.0 copy-start.7
  11.2 1.9 %collective-permute-start = (f32[24,2304]{1,0:T(8,128)}, f32[24,2304]{1,0:T(8,128)S(1)}, u32[]{:S(2)}, u32[]{:S(2)}) collective-permute-start(f32[24,2304]{1,0:T(8,128)} %get-tuple-element.20), channel_id=1, source_target_pairs={{0,32},{32,64},{64,96},{96,128},{128,160},{160,192},{192,224},{224... | collective-permute-start | bytes 663560 | tf_op jit(solution)/shard_map/ppermute | solution.py:431
  13.1 0.0 copy-done.6
  13.1 0.0 copy-done.7
  13.1 0.0 copy-start.4
  13.1 1.0 copy-done.4
  14.1 0.0 copy-start.5
  14.2 5.4 %collective-permute-done.behind_ref = f32[24,2304]{1,0:T(8,128)S(1)} collective-permute-done((f32[24,2304]{1,0:T(8,128)}, f32[24,2304]{1,0:T(8,128)S(1)}, u32[]{:S(2)}, u32[]{:S(2)}) %collective-permute-start) | collective-permute-done | bytes 221216 | tf_op jit(solution)/shard_map/ppermute | solution.py:431
  19.5 0.0 copy-done
  19.6 0.0 copy-done.5
  19.6 1.9 %first_relax.1 = f32[32,1,4608]{2,1,0:T(1,128)S(1)} custom-call(s32[1]{0:T(128)} %bitcast.rank_ref, f32[48,2304]{1,0:T(8,128)S(1)} %get-tuple-element.19.density_ref, f32[24,2304]{1,0:T(8,128)S(1)} %collective-permute-done.behind_ref, f32[1,2304]{1,0:T(1,128)S(1)} %copy-done.5, bf16[3,512,256]{2,1,0:T(8,128)(2,1)S(1)} %copy-done), custom_call_target="tpu_custom_call" | custom-call | tf_op jit(solution)/shard_map/first_relax/pallas_call | solution.py:441
  21.5 32.0 %all_to_all.20 = f32[32,1,4608]{2,1,0:T(1,128)S(1)} all-to-all(f32[32,1,4608]{2,1,0:T(1,128)S(1)} %first_relax.1), channel_id=1, replica_groups=mesh['dom'=16,'orb'=32] {'orb'}, dimensions={0} | all-to-all | bytes 1179648 | tf_op jit(solution)/shard_map/all_to_all | solution.py:450
  53.5 0.3 reduce_sum.22
  53.8 0.1 fusion
  53.9 0.2 broadcast_in_dim.9
  54.1 0.0 copy-start.3
  54.1 21.3 %all_to_all.21 = f32[32,1,2304]{2,1,0:T(1,128)S(1)} all-to-all(f32[32,1,2304]{2,1,0:T(1,128)S(1)} %broadcast_in_dim.9), channel_id=1, replica_groups=mesh['dom'=16,'orb'=32] {'orb'}, dimensions={0} | all-to-all | bytes 589824 | tf_op jit(solution)/shard_map/all_to_all | solution.py:454
  75.5 0.0 copy-start.1
  75.5 0.0 copy-start.2
  75.5 2.1 %collective-permute-start.1 = (f32[21,2304]{1,0:T(8,128)S(1)}, f32[21,2304]{1,0:T(8,128)S(1)}, u32[]{:S(2)}, u32[]{:S(2)}) collective-permute-start(f32[21,2304]{1,0:T(8,128)S(1)} %pad_maximum_fusion), channel_id=1, source_target_pairs={{32,0},{64,32},{96,64},{128,96},{160,128},{192,160},{224,192},{256... | collective-permute-start | bytes 580616 | tf_op jit(solution)/shard_map/ppermute | solution.py:456
  77.6 3.4 %collective-permute-done.1.high_ref = f32[21,2304]{1,0:T(8,128)S(1)} collective-permute-done((f32[21,2304]{1,0:T(8,128)S(1)}, f32[21,2304]{1,0:T(8,128)S(1)}, u32[]{:S(2)}, u32[]{:S(2)}) %collective-permute-start.1) | collective-permute-done | bytes 193568 | tf_op jit(solution)/shard_map/ppermute | solution.py:456
  81.0 0.0 copy-done.3
  81.0 0.0 copy-done.1
  81.0 0.0 copy-done.2
  81.0 7.3 %second_filter.1 = (f32[48,2304]{1,0:T(8,128)S(1)}, f32[16,2304]{1,0:T(8,128)S(1)}, f32[16,2304]{1,0:T(8,128)S(1)}, f32[16,1,128]{2,1,0:T(1,128)S(1)}) custom-call(s32[1]{0:T(128)} %bitcast.rank_ref, s32[1]{0:T(128)S(6)} %copy.16.count_ref, f32[1,2]{1,0:T(1,128)S(1)} %get-tuple-element.16.occupation_ref, f32[2,56,2304]{2,1,0:T(8,128)S(1)} %copy-done.3, ...), custom_call_target="tpu_custom_call" | custom-call | tf_op jit(solution)/shard_map/second_filter/pallas_call | solution.py:458
  88.4 5.4 %collective-permute-start.2 = (f32[16,2304]{1,0:T(8,128)S(1)}, f32[16,2304]{1,0:T(8,128)S(1)}, u32[]{:S(2)}, u32[]{:S(2)}) collective-permute-start(f32[16,2304]{1,0:T(8,128)S(1)} %get-tuple-element.22), channel_id=1, source_target_pairs={{0,32},{32,64},{64,96},{96,128},{128,160},{160,192},{192,224},{224... | collective-permute-start | bytes 442376 | tf_op jit(solution)/shard_map/ppermute | solution.py:472
  93.8 1.9 %collective-permute-start.3 = (f32[16,2304]{1,0:T(8,128)S(1)}, f32[16,2304]{1,0:T(8,128)S(1)}, u32[]{:S(2)}, u32[]{:S(2)}) collective-permute-start(f32[16,2304]{1,0:T(8,128)S(1)} %get-tuple-element.23), channel_id=1, source_target_pairs={{32,0},{64,32},{96,64},{128,96},{160,128},{192,160},{224,192},{256... | collective-permute-start | bytes 442376 | tf_op jit(solution)/shard_map/ppermute | solution.py:473
  95.7 12.4 %all_to_all.22 = f32[16,1,128]{2,1,0:T(1,128)S(1)} all-to-all(f32[16,1,128]{2,1,0:T(1,128)S(1)} %get-tuple-element.24), channel_id=1, replica_groups=mesh['dom'=16,'orb'=32] {'dom'}, dimensions={0} | all-to-all | bytes 16384 | tf_op jit(solution)/shard_map/all_to_all | solution.py:471
  108.1 0.0 collective-permute-done.2.below_ref
  108.1 0.0 collective-permute-done.3.above_ref
  108.1 1.9 %second_relax.1 = f32[32,1,4736]{2,1,0:T(1,128)S(1)} custom-call(s32[1]{0:T(128)} %bitcast.rank_ref, f32[48,2304]{1,0:T(8,128)S(1)} %get-tuple-element.21.density_ref, f32[16,2304]{1,0:T(8,128)S(1)} %collective-permute-done.2.below_ref, f32[16,2304]{1,0:T(8,128)S(1)} %collective-permute-done.3.above_ref, f32[1,2304]{1,0:T(1,128)S(1)} %get-tuple-element.27.plane_ref, ...), custom_call_target="tpu_custom_call" | custom-call | tf_op jit(solution)/shard_map/second_relax/pallas_call | solution.py:474
  110.1 26.8 %all_to_all.23.arrived_ref = f32[32,1,4736]{2,1,0:T(1,128)S(1)} all-to-all(f32[32,1,4736]{2,1,0:T(1,128)S(1)} %second_relax.1), channel_id=1, replica_groups=mesh['dom'=16,'orb'=32] {'orb'}, dimensions={0} | all-to-all | bytes 1212416 | tf_op jit(solution)/shard_map/all_to_all | solution.py:483
  136.9 0.7 last.1
  (7 shorter events, 0.2 us)
Async XLA Ops:
  0.7 18.9 %copy-start = (bf16[3,512,256]{2,1,0:T(8,128)(2,1)S(1)}, bf16[3,512,256]{2,1,0:T(8,128)(2,1)}, u32[]{:S(2)}) copy-start(bf16[3,512,256]{2,1,0:T(8,128)(2,1)} %constant.10.clone.matrix_hbm.matrix_ref) | copy-start | bytes 2359300
  11.2 2.0 %copy-start.6 = (f32[1,2]{1,0:T(1,128)S(1)}, f32[1,2]{1,0:T(1,128)}, u32[]{:S(2)}) copy-start(f32[1,2]{1,0:T(1,128)} %occupation_ref.3) | copy-start | bytes 28
  11.2 2.0 %copy-start.7 = (f32[1,48]{1,0:T(1,128)S(1)}, f32[1,48]{1,0:T(1,128)}, u32[]{:S(2)}) copy-start(f32[1,48]{1,0:T(1,128)} %weight_ref.3) | copy-start | bytes 580
  11.2 8.4 %collective-permute-start = (f32[24,2304]{1,0:T(8,128)}, f32[24,2304]{1,0:T(8,128)S(1)}, u32[]{:S(2)}, u32[]{:S(2)}) collective-permute-start(f32[24,2304]{1,0:T(8,128)} %get-tuple-element.20), channel_id=1, source_target_pairs={{0,32},{32,64},{64,96},{96,128},{128,160},{160,192},{192,224},{224... | collective-permute-start | bytes 663560 | tf_op jit(solution)/shard_map/ppermute | solution.py:431
  13.1 1.0 copy-start.4
  14.1 5.4 %copy-start.5 = (f32[1,2304]{1,0:T(1,128)S(1)}, f32[1,2304]{1,0:T(1,128)}, u32[]{:S(2)}) copy-start(f32[1,2304]{1,0:T(1,128)} %guess_ref.3) | copy-start | bytes 27652
  54.1 26.9 %copy-start.3 = (f32[2,56,2304]{2,1,0:T(8,128)S(1)}, f32[2,56,2304]{2,1,0:T(8,128)}, u32[]{:S(2)}) copy-start(f32[2,56,2304]{2,1,0:T(8,128)} %get-tuple-element.17.psi_ref) | copy-start | bytes 3096580
  75.5 5.6 %copy-start.1 = (f32[1,48,2304]{2,1,0:T(8,128)S(1)}, f32[1,48,2304]{2,1,0:T(8,128)}, u32[]{:S(2)}) copy-start(f32[1,48,2304]{2,1,0:T(8,128)} %ext_ref.1) | copy-start | bytes 1327108
  75.5 5.5 %copy-start.2 = (f32[1,48,2304]{2,1,0:T(8,128)S(1)}, f32[1,48,2304]{2,1,0:T(8,128)}, u32[]{:S(2)}) copy-start(f32[1,48,2304]{2,1,0:T(8,128)} %core_ref.1) | copy-start | bytes 1327108
  75.5 5.5 %collective-permute-start.1 = (f32[21,2304]{1,0:T(8,128)S(1)}, f32[21,2304]{1,0:T(8,128)S(1)}, u32[]{:S(2)}, u32[]{:S(2)}) collective-permute-start(f32[21,2304]{1,0:T(8,128)S(1)} %pad_maximum_fusion), channel_id=1, source_target_pairs={{32,0},{64,32},{96,64},{128,96},{160,128},{192,160},{224,192},{256... | collective-permute-start | bytes 580616 | tf_op jit(solution)/shard_map/ppermute | solution.py:456
  88.4 19.8 %collective-permute-start.2 = (f32[16,2304]{1,0:T(8,128)S(1)}, f32[16,2304]{1,0:T(8,128)S(1)}, u32[]{:S(2)}, u32[]{:S(2)}) collective-permute-start(f32[16,2304]{1,0:T(8,128)S(1)} %get-tuple-element.22), channel_id=1, source_target_pairs={{0,32},{32,64},{64,96},{96,128},{128,160},{160,192},{192,224},{224... | collective-permute-start | bytes 442376 | tf_op jit(solution)/shard_map/ppermute | solution.py:472
  93.8 14.4 %collective-permute-start.3 = (f32[16,2304]{1,0:T(8,128)S(1)}, f32[16,2304]{1,0:T(8,128)S(1)}, u32[]{:S(2)}, u32[]{:S(2)}) collective-permute-start(f32[16,2304]{1,0:T(8,128)S(1)} %get-tuple-element.23), channel_id=1, source_target_pairs={{32,0},{64,32},{96,64},{128,96},{160,128},{192,160},{224,192},{256... | collective-permute-start | bytes 442376 | tf_op jit(solution)/shard_map/ppermute | solution.py:473

commit v5 on v4

--- a/solution.py
+++ b/solution.py
@@ -202,7 +202,7 @@
     ]
 
 
-def density_tile(a_refs, scale, factor, core_ref, weight_ref, t, share):
+def density_tile(a_refs, scale, factor, core_ref, weight_ref, t, share, psi_out):
     row = lax.broadcasted_iota(jnp.int32, (8, BOX), 0)
     column = lax.broadcasted_iota(jnp.int32, (8, BOX), 1)
     weight = jnp.where(column == row + 8 * t, jnp.broadcast_to(weight_ref[...], (8, BOX)), 0.0)
@@ -210,6 +210,8 @@
     total = [share * c for c in tile_of(core_ref, 8 * t)]
     for q, ref in enumerate(a_refs):
         y = [p * scale[q] for p in tile_of(ref, PAD + 8 * t)]
+        if psi_out is not None:
+            put_tile(psi_out.at[q], 8 * t, y)
         total = [total[i] + factor[q] * (y[i] * y[i]) for i in range(COLS)]
     return [weight * d for d in total]
 
@@ -238,9 +240,9 @@
 def first_filter(
     orb_count, rank_ref, count_ref, occupation_ref, orbitals_ref, ext_ref, core_ref, matrix_hbm, weight_ref, guess_ref,
     psi_out, density_out, up_out,
-    a0, a1, b0, b1, x0, x1, s0, s1, w_ref, matrix_ref, v_ref, c_ref, scale_ref, sem,
+    a0, a1, b0, b1, x0, x1, s0, s1, w_ref, matrix_ref, v_ref, c_ref, sem,
 ):
-    third = BOX // 3
+    third = BOX
     copies = []
     for n, (source, target, first) in enumerate((
         (ext_ref.at[0], v_ref, 0), (orbitals_ref.at[0, 0], a0, PAD), (orbitals_ref.at[0, 1], a1, PAD),
@@ -251,12 +253,15 @@
                 source.at[third * k : third * (k + 1)], target.at[first + third * k : first + third * (k + 1)],
                 sem.at[n, k],
             )
-            for k in range(3)
+            for k in range(1)
         ])
-    copies.append([pltpu.make_async_copy(matrix_hbm.at[k], matrix_ref.at[k], sem.at[4, k]) for k in range(3)])
-    for n in (0, 1, 4, 2, 3):
-        for copy in copies[n]:
-            copy.start()
+    copies.append([pltpu.make_async_copy(matrix_hbm, matrix_ref, sem.at[4, 0])])
+    def begin(*wanted):
+        for n in wanted:
+            for copy in copies[n]:
+                copy.start()
+
+    begin(0, 1, 2, 4)
 
     def arrived(n):
         for copy in copies[n]:
@@ -265,28 +270,17 @@
     clear_pads((a0, a1, b0, b1), BOX)
     arrived(0)
     single = scaled_potential(lambda r: tile_of(v_ref, r), w_ref)
-    for n in (1, 4, 2):
+    for n in (1, 2, 4):
         arrived(n)
+    begin(3)
     run_filter((a0, a1), (b0, b1), (x0, x1), (s0, s1), matrix_ref, w_ref, single)
-    leaving = [
-        pltpu.make_async_copy(ref.at[PAD : PAD + BOX], psi_out.at[q, 0:BOX], sem.at[5, q])
-        for q, ref in enumerate((a0, a1))
-    ]
-    for copy in leaving:
-        copy.start()
     scale = norms((a0, a1))
-    for q in range(2):
-        put_tile(scale_ref, 8 * q, [scale[q]] * COLS)
-        leaving.append(pltpu.make_async_copy(scale_ref.at[8 * q : 8 * q + 8], psi_out.at[q, BOX : BOX + 8], sem.at[6, q]))
-        leaving[-1].start()
     factor = occupation_factors(rank_ref, count_ref, occupation_ref, 2, 2 * orb_count)
     arrived(3)
     for t in range(BOX // 8):
-        put_tile(density_out, 8 * t, density_tile((a0, a1), scale, factor, c_ref, weight_ref, t, 1.0 / orb_count))
+        put_tile(density_out, 8 * t, density_tile((a0, a1), scale, factor, c_ref, weight_ref, t, 1.0 / orb_count, psi_out))
     up_out[0:1, :] = guess_ref[...]
     up_out[1:24, :] = density_out[25:48, :]
-    for copy in leaving:
-        copy.wait()
 
 
 def first_relax(rank_ref, density_ref, behind_ref, guess_ref, matrix_ref, out_ref, g_ref, h_ref, d_ref, x0, s0):
@@ -320,10 +314,8 @@
     a0, a1, b0, b1, x0, x1, s0, s1, w_ref, v_ref,
 ):
     clear_pads((a0, a1, b0, b1), BOX)
-    for q, ref in enumerate((a0, a1)):
-        scale = tile_of(psi_ref.at[q], BOX)[0]
-        for t in range(BOX // 8):
-            put_tile(ref, PAD + 8 * t, [y * scale for y in tile_of(psi_ref.at[q], 8 * t)])
+    a0[PAD : PAD + BOX, :] = psi_ref[0]
+    a1[PAD : PAD + BOX, :] = psi_ref[1]
     first = SHIFT - BUF
     v_ref[0 : CORE - first, :] = low_ref[first:CORE, :]
     v_ref[CORE - first : BOX, :] = high_ref[0:UP, :]
@@ -337,7 +329,7 @@
     factor = occupation_factors(rank_ref, count_ref, occupation_ref, 2, 2 * orb_count)
     charge = [jnp.zeros((8, LANES), jnp.float32) for _ in range(3)]
     for t in range(BOX // 8):
-        tile = density_tile((a0, a1), scale, factor, core_ref, weight_ref, t, 1.0 / orb_count)
+        tile = density_tile((a0, a1), scale, factor, core_ref, weight_ref, t, 1.0 / orb_count, None)
         put_tile(density_out, 8 * t, tile)
         for i, d in enumerate(tile):
             charge[i % 3] = charge[i % 3] + d
@@ -420,10 +412,9 @@
     psi, density, upper = pl.pallas_call(
         functools.partial(first_filter, orb_count),
         in_specs=[SMEM] * 3 + [HBM] * 4 + [VMEM] * 2,
-        out_specs=[HBM] + [VMEM] * 2,
-        out_shape=[f32(per_device, BOX + 8, CELLS), f32(BOX, CELLS), f32(24, CELLS)],
-        scratch_shapes=filter_scratch
-        + [whole, box, box, pltpu.VMEM((16, CELLS), jnp.float32), pltpu.SemaphoreType.DMA((7, 3))],
+        out_specs=[VMEM] * 3,
+        out_shape=[f32(per_device, BOX, CELLS), f32(BOX, CELLS), f32(24, CELLS)],
+        scratch_shapes=filter_scratch + [whole, box, box, pltpu.SemaphoreType.DMA((5, 3))],
         compiler_params=pltpu.CompilerParams(vmem_limit_bytes=FIRST),
         name="first_filter",
     )(place, occupied_count, occupations, orbitals, external_potential, core_density, matrix, weights, hartree_guess)

time: 138 us -> 137 us (level)
  the two profiles are of different devices: /device:TPU:2 before, /device:TPU:64 now
where the time goes in v5:
time: 137 us
  blocking collectives  87.4 us (64%)
  Pallas kernels  21.8 us (16%)
  starting transfers between devices  14.8 us (11%)
  waiting for transfers between devices  9.98 us (7%)
    all_to_all x1, blocking collectives, body(): total = lax.all_to_all(sent, 'orb', 0, 0, tiled=True).sum(axis=0)  32.2 us
    all_to_all x1, blocking collectives, body(): arrived = lax.all_to_all(sent, 'orb', 0, 0, tiled=True)  27.6 us
    all_to_all x1, blocking collectives, body(): lax.all_to_all(jnp.broadcast_to(plane[None], (orb_count, 1, CELLS)), 'orb...  19.1 us
    pallas_call x1, Pallas kernels, body(): pl.pallas_call(functools.partial(first_filter, orb_count), in_specs=[SMEM...  10 us
    all_to_all x1, blocking collectives, body(): charge = lax.all_to_all(charge, 'dom', 0, 0, tiled=True).sum(axis=0)  8.6 us
    pallas_call x1, Pallas kernels, body(): pl.pallas_call(functools.partial(second_filter, orb_count), in_specs=[SME...  7.29 us
    ppermute x1, waiting for transfers between devices, body(): behind = lax.ppermute(upper, 'dom', up)  6.57 us
    ppermute x1, starting transfers between devices, body(): from_above = lax.ppermute(lower, 'dom', down)  5.94 us
  transfers between devices with their start and end apart: 4, of which 2 were waited for; matrix products, arithmetic and copies ran while one was open for 0% of the time, Pallas kernels for 0%

profile of v5, /device:TPU:64, one launch (start us, length us, event | category | flops | bytes accessed | tf_op | source)
XLA Modules:
  0.0 136.7 jit_solution(16894260154685277663)
XLA Ops:
  0.7 0.0 copy-start
  0.7 10.0 %first_filter.1 = (f32[2,48,2304]{2,1,0:T(8,128)}, f32[48,2304]{1,0:T(8,128)}, f32[24,2304]{1,0:T(8,128)}) custom-call(s32[1]{0:T(128)} %bitcast.rank_ref, s32[1]{0:T(128)S(6)} %copy.16.count_ref, f32[1,2]{1,0:T(1,128)} %occupation_ref.3, f32[1,2,48,2304]{3,2,1,0:T(8,128)} %orbitals_ref.1, f32[1,48,2304]{2,1,0:T(8,128)} %ext_ref.1, f32[1,48,2304]{2,1,0:T(8,128)} %core_ref.1, ...), custom_call_target="tpu_custom_call" | custom-call | tf_op jit(solution)/shard_map/first_filter/pallas_call | solution.py:412
  10.7 0.0 copy-start.6
  10.7 0.0 copy-start.7
  10.7 1.9 %collective-permute-start = (f32[24,2304]{1,0:T(8,128)}, f32[24,2304]{1,0:T(8,128)S(1)}, u32[]{:S(2)}, u32[]{:S(2)}) collective-permute-start(f32[24,2304]{1,0:T(8,128)} %get-tuple-element.20), channel_id=1, source_target_pairs={{0,32},{32,64},{64,96},{96,128},{128,160},{160,192},{192,224},{224... | collective-permute-start | bytes 663560 | tf_op jit(solution)/shard_map/ppermute | solution.py:422
  12.6 0.0 copy-done.6
  12.6 0.0 copy-done.7
  12.7 0.0 copy-start.4
  12.7 1.0 copy-done.4
  13.7 0.0 copy-start.5
  13.7 6.6 %collective-permute-done.behind_ref = f32[24,2304]{1,0:T(8,128)S(1)} collective-permute-done((f32[24,2304]{1,0:T(8,128)}, f32[24,2304]{1,0:T(8,128)S(1)}, u32[]{:S(2)}, u32[]{:S(2)}) %collective-permute-start) | collective-permute-done | bytes 221216 | tf_op jit(solution)/shard_map/ppermute | solution.py:422
  20.3 0.0 copy-done
  20.3 0.0 copy-done.5
  20.3 1.9 %first_relax.1 = f32[32,1,4608]{2,1,0:T(1,128)S(1)} custom-call(s32[1]{0:T(128)} %bitcast.rank_ref, f32[48,2304]{1,0:T(8,128)S(1)} %get-tuple-element.19.density_ref, f32[24,2304]{1,0:T(8,128)S(1)} %collective-permute-done.behind_ref, f32[1,2304]{1,0:T(1,128)S(1)} %copy-done.5, bf16[3,512,256]{2,1,0:T(8,128)(2,1)S(1)} %copy-done), custom_call_target="tpu_custom_call" | custom-call | tf_op jit(solution)/shard_map/first_relax/pallas_call | solution.py:432
  22.2 32.2 %all_to_all.20 = f32[32,1,4608]{2,1,0:T(1,128)S(1)} all-to-all(f32[32,1,4608]{2,1,0:T(1,128)S(1)} %first_relax.1), channel_id=1, replica_groups=mesh['dom'=16,'orb'=32] {'orb'}, dimensions={0} | all-to-all | bytes 1179648 | tf_op jit(solution)/shard_map/all_to_all | solution.py:441
  54.4 0.3 reduce_sum.22
  54.7 0.1 fusion
  54.8 0.2 broadcast_in_dim.9
  55.0 19.1 %all_to_all.21 = f32[32,1,2304]{2,1,0:T(1,128)S(1)} all-to-all(f32[32,1,2304]{2,1,0:T(1,128)S(1)} %broadcast_in_dim.9), channel_id=1, replica_groups=mesh['dom'=16,'orb'=32] {'orb'}, dimensions={0} | all-to-all | bytes 589824 | tf_op jit(solution)/shard_map/all_to_all | solution.py:445
  74.1 0.0 copy-start.3
  74.2 0.0 copy-start.1
  74.2 0.0 copy-start.2
  74.2 5.0 %collective-permute-start.1 = (f32[21,2304]{1,0:T(8,128)S(1)}, f32[21,2304]{1,0:T(8,128)S(1)}, u32[]{:S(2)}, u32[]{:S(2)}) collective-permute-start(f32[21,2304]{1,0:T(8,128)S(1)} %pad_maximum_fusion), channel_id=1, source_target_pairs={{32,0},{64,32},{96,64},{128,96},{160,128},{192,160},{224,192},{256... | collective-permute-start | bytes 580616 | tf_op jit(solution)/shard_map/ppermute | solution.py:447
  79.3 3.4 %collective-permute-done.1.high_ref = f32[21,2304]{1,0:T(8,128)S(1)} collective-permute-done((f32[21,2304]{1,0:T(8,128)S(1)}, f32[21,2304]{1,0:T(8,128)S(1)}, u32[]{:S(2)}, u32[]{:S(2)}) %collective-permute-start.1) | collective-permute-done | bytes 193568 | tf_op jit(solution)/shard_map/ppermute | solution.py:447
  82.7 0.0 copy-done.3
  82.7 0.0 copy-done.1
  82.7 0.0 copy-done.2
  82.7 7.3 %second_filter.1 = (f32[48,2304]{1,0:T(8,128)S(1)}, f32[16,2304]{1,0:T(8,128)S(1)}, f32[16,2304]{1,0:T(8,128)S(1)}, f32[16,1,128]{2,1,0:T(1,128)S(1)}) custom-call(s32[1]{0:T(128)} %bitcast.rank_ref, s32[1]{0:T(128)S(6)} %copy.16.count_ref, f32[1,2]{1,0:T(1,128)S(1)} %get-tuple-element.16.occupation_ref, f32[2,48,2304]{2,1,0:T(8,128)S(1)} %copy-done.3, ...), custom_call_target="tpu_custom_call" | custom-call | tf_op jit(solution)/shard_map/second_filter/pallas_call | solution.py:449
  90.0 1.9 %collective-permute-start.2 = (f32[16,2304]{1,0:T(8,128)S(1)}, f32[16,2304]{1,0:T(8,128)S(1)}, u32[]{:S(2)}, u32[]{:S(2)}) collective-permute-start(f32[16,2304]{1,0:T(8,128)S(1)} %get-tuple-element.22), channel_id=1, source_target_pairs={{0,32},{32,64},{64,96},{96,128},{128,160},{160,192},{192,224},{224... | collective-permute-start | bytes 442376 | tf_op jit(solution)/shard_map/ppermute | solution.py:463
  91.9 5.9 %collective-permute-start.3 = (f32[16,2304]{1,0:T(8,128)S(1)}, f32[16,2304]{1,0:T(8,128)S(1)}, u32[]{:S(2)}, u32[]{:S(2)}) collective-permute-start(f32[16,2304]{1,0:T(8,128)S(1)} %get-tuple-element.23), channel_id=1, source_target_pairs={{32,0},{64,32},{96,64},{128,96},{160,128},{192,160},{224,192},{256... | collective-permute-start | bytes 442376 | tf_op jit(solution)/shard_map/ppermute | solution.py:464
  97.9 8.6 %all_to_all.22 = f32[16,1,128]{2,1,0:T(1,128)S(1)} all-to-all(f32[16,1,128]{2,1,0:T(1,128)S(1)} %get-tuple-element.24), channel_id=1, replica_groups=mesh['dom'=16,'orb'=32] {'dom'}, dimensions={0} | all-to-all | bytes 16384 | tf_op jit(solution)/shard_map/all_to_all | solution.py:462
  106.5 0.0 collective-permute-done.2.below_ref
  106.5 0.0 collective-permute-done.3.above_ref
  106.5 1.9 %second_relax.1 = f32[32,1,4736]{2,1,0:T(1,128)S(1)} custom-call(s32[1]{0:T(128)} %bitcast.rank_ref, f32[48,2304]{1,0:T(8,128)S(1)} %get-tuple-element.21.density_ref, f32[16,2304]{1,0:T(8,128)S(1)} %collective-permute-done.2.below_ref, f32[16,2304]{1,0:T(8,128)S(1)} %collective-permute-done.3.above_ref, f32[1,2304]{1,0:T(1,128)S(1)} %get-tuple-element.27.plane_ref, ...), custom_call_target="tpu_custom_call" | custom-call | tf_op jit(solution)/shard_map/second_relax/pallas_call | solution.py:465
  108.4 27.6 %all_to_all.23.arrived_ref = f32[32,1,4736]{2,1,0:T(1,128)S(1)} all-to-all(f32[32,1,4736]{2,1,0:T(1,128)S(1)} %second_relax.1), channel_id=1, replica_groups=mesh['dom'=16,'orb'=32] {'orb'}, dimensions={0} | all-to-all | bytes 1212416 | tf_op jit(solution)/shard_map/all_to_all | solution.py:474
  136.0 0.7 last.1
  (7 shorter events, 0.2 us)
Async XLA Ops:
  0.7 19.6 %copy-start = (bf16[3,512,256]{2,1,0:T(8,128)(2,1)S(1)}, bf16[3,512,256]{2,1,0:T(8,128)(2,1)}, u32[]{:S(2)}) copy-start(bf16[3,512,256]{2,1,0:T(8,128)(2,1)} %constant.10.clone.matrix_hbm.matrix_ref) | copy-start | bytes 2359300
  10.7 2.0 %copy-start.6 = (f32[1,2]{1,0:T(1,128)S(1)}, f32[1,2]{1,0:T(1,128)}, u32[]{:S(2)}) copy-start(f32[1,2]{1,0:T(1,128)} %occupation_ref.3) | copy-start | bytes 28
  10.7 2.0 %copy-start.7 = (f32[1,48]{1,0:T(1,128)S(1)}, f32[1,48]{1,0:T(1,128)}, u32[]{:S(2)}) copy-start(f32[1,48]{1,0:T(1,128)} %weight_ref.3) | copy-start | bytes 580
  10.7 9.6 %collective-permute-start = (f32[24,2304]{1,0:T(8,128)}, f32[24,2304]{1,0:T(8,128)S(1)}, u32[]{:S(2)}, u32[]{:S(2)}) collective-permute-start(f32[24,2304]{1,0:T(8,128)} %get-tuple-element.20), channel_id=1, source_target_pairs={{0,32},{32,64},{64,96},{96,128},{128,160},{160,192},{192,224},{224... | collective-permute-start | bytes 663560 | tf_op jit(solution)/shard_map/ppermute | solution.py:422
  12.7 1.0 copy-start.4
  13.7 6.6 %copy-start.5 = (f32[1,2304]{1,0:T(1,128)S(1)}, f32[1,2304]{1,0:T(1,128)}, u32[]{:S(2)}) copy-start(f32[1,2304]{1,0:T(1,128)} %guess_ref.3) | copy-start | bytes 27652
  74.1 8.6 %copy-start.3 = (f32[2,48,2304]{2,1,0:T(8,128)S(1)}, f32[2,48,2304]{2,1,0:T(8,128)}, u32[]{:S(2)}) copy-start(f32[2,48,2304]{2,1,0:T(8,128)} %get-tuple-element.17.psi_ref) | copy-start | bytes 2654212
  74.2 8.5 %copy-start.1 = (f32[1,48,2304]{2,1,0:T(8,128)S(1)}, f32[1,48,2304]{2,1,0:T(8,128)}, u32[]{:S(2)}) copy-start(f32[1,48,2304]{2,1,0:T(8,128)} %ext_ref.1) | copy-start | bytes 1327108
  74.2 8.5 %copy-start.2 = (f32[1,48,2304]{2,1,0:T(8,128)S(1)}, f32[1,48,2304]{2,1,0:T(8,128)}, u32[]{:S(2)}) copy-start(f32[1,48,2304]{2,1,0:T(8,128)} %core_ref.1) | copy-start | bytes 1327108
  74.2 8.5 %collective-permute-start.1 = (f32[21,2304]{1,0:T(8,128)S(1)}, f32[21,2304]{1,0:T(8,128)S(1)}, u32[]{:S(2)}, u32[]{:S(2)}) collective-permute-start(f32[21,2304]{1,0:T(8,128)S(1)} %pad_maximum_fusion), channel_id=1, source_target_pairs={{32,0},{64,32},{96,64},{128,96},{160,128},{192,160},{224,192},{256... | collective-permute-start | bytes 580616 | tf_op jit(solution)/shard_map/ppermute | solution.py:447
  90.0 16.5 %collective-permute-start.2 = (f32[16,2304]{1,0:T(8,128)S(1)}, f32[16,2304]{1,0:T(8,128)S(1)}, u32[]{:S(2)}, u32[]{:S(2)}) collective-permute-start(f32[16,2304]{1,0:T(8,128)S(1)} %get-tuple-element.22), channel_id=1, source_target_pairs={{0,32},{32,64},{64,96},{96,128},{128,160},{160,192},{192,224},{224... | collective-permute-start | bytes 442376 | tf_op jit(solution)/shard_map/ppermute | solution.py:463
  91.9 14.6 %collective-permute-start.3 = (f32[16,2304]{1,0:T(8,128)S(1)}, f32[16,2304]{1,0:T(8,128)S(1)}, u32[]{:S(2)}, u32[]{:S(2)}) collective-permute-start(f32[16,2304]{1,0:T(8,128)S(1)} %get-tuple-element.23), channel_id=1, source_target_pairs={{32,0},{64,32},{96,64},{128,96},{160,128},{192,160},{224,192},{256... | collective-permute-start | bytes 442376 | tf_op jit(solution)/shard_map/ppermute | solution.py:464
